TPU v7x, 128 devices: a whole 4x4x4 slice. The times are simulated.
128 devices in a mesh: row: 8 (over z, core), col: 16 (over x, y).
Axes of the slice: x: 4, y: 4, z: 4, core: 2. Of those that a mesh axis runs over, the one named last changes fastest.
Arguments:
- form_rows: bfloat16 [4096, 64, 512], P(('row', 'col')), may hold values from -6 to 6
- form_strip: bfloat16 [16, 64, 512], P('col'), may hold values from -0.25 to 0.25
- lam_index: int32 [4096, 16, 8], P(('row', 'col')), may hold values from 0 to 15
- coef_index: int32 [4096, 16, 8], P(('row', 'col')), may hold values from 0 to 63
- term_count: int32 [4096, 16], P(('row', 'col')), may hold values from 1 to 8
- angular_coef: float32 [64], replicated, may hold values from -3 to 3
- kernels: float32 [16, 512], replicated, may hold values from 0.1 to 2
- pivots: int32 [512], replicated, may hold values from 0 to 262143, as said below
- lower_inverse: float32 [512, 512], replicated, as said below
- panel: bfloat16 [512, 262144], P('col', 'row'), may hold values from -0.25 to 0.25
Outputs:
- trailing: float32 [1024, 262144], P('col', 'row')
- upper_rows: bfloat16 [1024, 512], P('col')
Inputs may be any that keep to these rules, and one draw needn't show every extreme that they name: pivots are distinct strip rows; row 0 and row 262143 are always among them. lower_inverse is unit lower triangular.
All inputs are finite; a program needn't handle non-finite values.
Results may differ from a plain program's by a relative error of at most 0.0057.
Values may be sent and summed in bfloat16 or wider, within the bound.
No kernel may reach another device: no remote copies, remote signals or barrier semaphores. Data moves between devices by JAX's collectives and lax.ppermute only.
A program may use at most 192 MiB of HBM per device.

v0:
```python
import jax
import jax.numpy as jnp
from jax import lax
from jax.sharding import PartitionSpec as P


def term_weights(lam_index, coef_index, term_count, angular_coef, kernels):
    chans, strips, terms = lam_index.shape
    nlam = kernels.shape[0]
    ncoef = angular_coef.shape[0]
    position = lax.broadcasted_iota(jnp.int32, lam_index.shape, 2)
    live = (position < term_count[:, :, None]).astype(jnp.float32)
    coef_table = (coef_index[..., None] == jnp.arange(ncoef, dtype=jnp.int32)).astype(jnp.float32)
    coef_value = jnp.sum(coef_table * angular_coef, axis=-1)
    lam_table = (lam_index[..., None] == jnp.arange(nlam, dtype=jnp.int32)).astype(jnp.float32)
    mixing = jnp.sum((live * coef_value)[..., None] * lam_table, axis=2)
    radial = jnp.dot(mixing.reshape(chans * strips, nlam), kernels, precision=lax.Precision.HIGHEST)
    return radial.reshape(chans, strips, kernels.shape[1])


def shards(
    form_rows,
    form_strip,
    lam_index,
    coef_index,
    term_count,
    angular_coef,
    kernels,
    pivots,
    lower_inverse,
    panel,
):
    radial = term_weights(lam_index, coef_index, term_count, angular_coef, kernels)
    scaled = (form_rows.astype(jnp.float32)[:, None] * radial[:, :, None, :]).astype(jnp.bfloat16)
    result = jnp.einsum(
        "ijkr,jlr->ikjl",
        scaled,
        lax.all_gather(form_strip, "col", axis=0, tiled=True),
        preferred_element_type=jnp.float32,
    )
    assembled = result.astype(jnp.bfloat16)
    chans, nmom, nstrip, _ = assembled.shape
    nrow = lax.axis_size("row")
    ncol = lax.axis_size("col")
    scols = nstrip * nmom
    width = scols // ncol
    flat = assembled.reshape(chans * nmom, scols)
    channel = pivots // nmom
    moment = pivots % nmom
    grid_blocks = flat.reshape(chans // nrow, nrow, nmom, ncol, width).transpose(1, 3, 0, 2, 4)
    moved = lax.all_to_all(
        grid_blocks.reshape(nrow * ncol, chans // nrow, nmom, width),
        ("row", "col"),
        split_axis=0,
        concat_axis=0,
        tiled=True,
    )
    local_rows = moved.reshape(-1, width).T
    owner = channel % nrow
    place = channel // nrow * nmom + moment
    taken = jnp.take(local_rows, place, axis=1).astype(jnp.float32)
    picked = jnp.where((owner == lax.axis_index("row"))[None, :], taken, 0.0)
    chosen_t = lax.psum(picked.astype(jnp.bfloat16), "row").astype(jnp.float32)
    upper_t = jnp.dot(chosen_t, lower_inverse.T, precision=lax.Precision.HIGHEST).astype(
        jnp.bfloat16
    )
    update = jnp.dot(
        upper_t,
        lax.all_gather(panel, "col", axis=0, tiled=True),
        preferred_element_type=jnp.float32,
    )
    trailing = local_rows.astype(jnp.float32) - update
    return (trailing, upper_t)


def solution(mesh):
    in_specs = (
        P(("row", "col"), None, None),
        P("col", None, None),
        P(("row", "col"), None, None),
        P(("row", "col"), None, None),
        P(("row", "col"), None),
        P(),
        P(),
        P(),
        P(),
        P("col", "row"),
    )
    out_specs = (P("col", "row"), P("col", None))
    return jax.shard_map(shards, mesh=mesh, in_specs=in_specs, out_specs=out_specs, check_vma=False)
```

profile of v0, /device:TPU:1, one launch (start us, length us, event | category | flops | bytes accessed | tf_op | source)
XLA Modules:
  0.0 455.3 jit_solution(4088146526022882842)
XLA Ops:
  7.2 0.0 copy-start
  7.2 0.0 copy-start.2
  7.2 0.0 all-gather.3.cloned.1.call-start
  7.2 0.7 all-gather.3.cloned.1.call-update
  7.9 4.1 convert_element_type.28
  12.0 1.0 copy.29
  13.0 0.8 copy.28
  13.8 2.0 select_reduce_fusion
  15.8 0.1 fusion.5
  15.9 0.2 copy.30
  16.1 1.0 select_reduce_fusion.1
  17.1 0.0 copy-done.2
  17.1 1.0 fusion.7
  18.2 36.4 %all-gather.3.cloned.1.call-done = bf16[16,64,512]{2,1,0:T(8,128)(2,1)} async-done(((bf16[1,64,512]{2,1,0:T(8,128)(2,1)}), bf16[16,64,512]{2,1,0:T(8,128)(2,1)}) %all-gather.3.cloned.1.call-update) | async-done | bytes 1048592 | tf_op jit(solution)/shard_map/all_gather | solution.py:38
  54.6 12.6 %fusion.3 = bf16[16,32,64,64]{3,2,1,0:T(8,128)(2,1)} fusion(f32[32,16,512]{2,0,1:T(8,128)S(1)} %fusion.7, f32[32,64,512]{2,1,0:T(8,128)} %convert_element_type.28, bf16[16,64,512]{2,1,0:T(8,128)(2,1)} %all-gather.3.cloned.1.call-done), kind=kOutput, calls=%fused_computation.6 | convolution fusion | flops 2183135232 | bytes 10485760 | tf_op jit(solution)/shard_map/ijkr,jlr->ikjl/dot_general | solution.py:35
  67.2 9.6 %copy.31 = bf16[4,8,64,16,64]{4,2,0,3,1:T(8,128)(2,1)} copy(bf16[4,8,64,16,64]{4,2,1,0,3:T(8,128)(2,1)} %bitcast.29) | data formatting | bytes 8388608 | tf_op jit(solution)/shard_map/reshape;reshape | solution.py:50
  76.8 0.0 copy-start.3
  76.8 14.3 %reshape.49 = bf16[128,2,8192]{2,1,0:T(2,128)(2,1)} reshape(bf16[128,4,64,64]{3,2,1,0:T(8,128)(2,1)} %bitcast.28) | data formatting | bytes 8388608
  91.1 9.4 %all-to-all-start = ((bf16[128,2,8192]{2,1,0:T(2,128)(2,1)}), bf16[128,2,8192]{2,1,0:T(2,128)(2,1)}, u32[]{:S(2)}, u32[]{:S(2)}) async-start(bf16[128,2,8192]{2,1,0:T(2,128)(2,1)} %reshape.49), calls=%async_computation | async-start | bytes 8388608 | tf_op jit(solution)/shard_map/all_to_all | solution.py:51
  100.6 0.2 all-reduce.2.cloned.1.call-start
  100.8 0.0 copy-done.3
  100.9 52.0 %all-to-all-done = bf16[128,2,8192]{2,1,0:T(2,128)(2,1)} async-done(((bf16[128,2,8192]{2,1,0:T(2,128)(2,1)}), bf16[128,2,8192]{2,1,0:T(2,128)(2,1)}, u32[]{:S(2)}, u32[]{:S(2)}) %all-to-all-start) | async-done | bytes 4194336 | tf_op jit(solution)/shard_map/all_to_all | solution.py:51
  152.9 14.6 %reshape.50 = bf16[128,4,64,64]{3,2,1,0:T(8,128)(2,1)} reshape(bf16[128,2,8192]{2,1,0:T(2,128)(2,1)} %all-to-all-done) | data formatting | bytes 8388608
  167.5 5.5 %gather_fusion = bf16[512,64]{1,0:T(8,128)(2,1)S(1)} fusion(bf16[64,32768]{0,1:T(8,128)(2,1)} %bitcast.26, s32[1024]{0:T(1024)S(1)} %pad_clamp_fusion), kind=kCustom, calls=%fused_computation | custom fusion | bytes 133120 | tf_op jit(solution)/shard_map/jit(_take)/gather | solution.py:61
  173.0 0.8 fusion.6
  173.9 0.0 all-reduce.2.cloned.1.call-update
  173.9 0.0 all-gather.5.cloned.1.call-start
  173.9 0.7 all-gather.5.cloned.1.call-update
  174.6 8.5 %copy.35 = bf16[32768,64]{0,1:T(8,128)(2,1)} copy(bf16[32768,64]{1,0:T(8,128)(2,1)} %bitcast.27) | data formatting | bytes 8388608 | tf_op jit(solution)/shard_map/reshape | solution.py:58
  183.2 44.2 %all-reduce.2.cloned.1.call-done = bf16[64,512]{0,1:T(8,128)(2,1)} async-done(((bf16[64,512]{0,1:T(8,128)(2,1)}), bf16[64,512]{0,1:T(8,128)(2,1)}) %all-reduce.2.cloned.1.call-update) | async-done | bytes 65552 | tf_op jit(solution)/shard_map/psum | solution.py:63
  227.4 0.0 copy-done
  227.4 1.6 convolution_convert_fusion
  229.0 0.0 copy-start.1
  229.0 198.7 %all-gather.5.cloned.1.call-done = bf16[512,32768]{1,0:T(8,128)(2,1)} async-done(((bf16[32,32768]{1,0:T(8,128)(2,1)}), bf16[512,32768]{1,0:T(8,128)(2,1)}) %all-gather.5.cloned.1.call-update) | async-done | bytes 33554448 | tf_op jit(solution)/shard_map/all_gather | solution.py:69
  427.7 21.1 %convolution_subtract_fusion = f32[64,32768]{1,0:T(8,128)} fusion(bf16[64,512]{1,0:T(8,128)(2,1)S(1)} %convolution_convert_fusion, bf16[512,32768]{1,0:T(8,128)(2,1)} %all-gather.5.cloned.1.call-done, bf16[32768,64]{0,1:T(8,128)(2,1)} %copy.35), kind=kOutput, calls=%fused_computation.2 | convolution fusion | flops 2151677952 | bytes 46202880 | tf_op jit(solution)/shard_map/dot_general | solution.py:67
  448.8 0.0 copy-done.1
  (2 shorter events, 0.0 us)
Async XLA Ops:
  7.2 220.2 %copy-start = (f32[512,512]{1,0:T(8,128)S(1)}, f32[512,512]{1,0:T(8,128)}, u32[]{:S(2)}) copy-start(f32[512,512]{1,0:T(8,128)} %param.18) | copy-start | bytes 3145732
  7.2 9.9 %copy-start.2 = (f32[16,512]{1,0:T(8,128)S(1)}, f32[16,512]{1,0:T(8,128)}, u32[]{:S(2)}) copy-start(f32[16,512]{1,0:T(8,128)} %param.16) | copy-start | bytes 98308
  7.2 47.4 %all-gather.3.cloned.1.call-start = ((), (), s32[]{:S(2)}) async-start(), calls=%async_computation.1 | async-start | bytes 1114112 | tf_op jit(solution)/shard_map/all_gather | solution.py:38
  76.8 24.0 %copy-start.3 = (s32[512]{0:T(512)S(1)}, s32[512]{0:T(512)}, u32[]{:S(2)}) copy-start(s32[512]{0:T(512)} %param.17) | copy-start | bytes 6148
  91.1 61.8 %all-to-all-start = ((bf16[128,2,8192]{2,1,0:T(2,128)(2,1)}), bf16[128,2,8192]{2,1,0:T(2,128)(2,1)}, u32[]{:S(2)}, u32[]{:S(2)}) async-start(bf16[128,2,8192]{2,1,0:T(2,128)(2,1)} %reshape.49), calls=%async_computation | async-start | bytes 8388608 | tf_op jit(solution)/shard_map/all_to_all | solution.py:51
  100.6 126.8 %all-reduce.2.cloned.1.call-start = ((), (), s32[]{:S(2)}) async-start(), calls=%async_computation.2 | async-start | bytes 262144 | tf_op jit(solution)/shard_map/psum | solution.py:63
  173.9 253.8 %all-gather.5.cloned.1.call-start = ((), (), s32[]{:S(2)}) async-start(), calls=%async_computation.3 | async-start | bytes 35651584 | tf_op jit(solution)/shard_map/all_gather | solution.py:69
  229.0 219.8 %copy-start.1 = (bf16[64,512]{1,0:T(8,128)(2,1)}, bf16[64,512]{1,0:T(8,128)(2,1)S(1)}, u32[]{:S(2)}) copy-start(bf16[64,512]{1,0:T(8,128)(2,1)S(1)} %convolution_convert_fusion) | copy-start | bytes 196612
Sparse Core Ops, SparseCore 0:
  10.2 44.3 all-gather.2
  174.0 53.3 all-reduce.1
  229.8 197.9 all-gather.4
where the time goes:
time: 457 us; the launch traced here: 455 us
  waiting for transfers between devices  333 us (73%)
  local copies, waits for them, and re-layouts  54.5 us (12%)
  matrix products  36.3 us (8%)
  between operations  13.9 us (3%)
  starting transfers between devices  9.75 us (2%)
  other arithmetic  8.09 us (2%)
    all_gather x1, waiting for transfers between devices, shards(): lax.all_gather(panel, 'col', axis=0, tiled=True)  199 us
    all_to_all x1, waiting for transfers between devices, shards(): lax.all_to_all(grid_blocks.reshape(nrow * ncol, chans // nrow, nmom, widt...  52 us
    psum x1, waiting for transfers between devices, shards(): chosen_t = lax.psum(picked.astype(jnp.bfloat16), 'row').astype(jnp.float32)  44.2 us
    all_gather x1, waiting for transfers between devices, shards(): lax.all_gather(form_strip, 'col', axis=0, tiled=True)  36.4 us
    unnamed x12, local copies, waits for them, and re-layouts  30.7 us
    dot_general x1, matrix products, shards(): jnp.dot(upper_t, lax.all_gather(panel, 'col', axis=0, tiled=True), prefer...  21.1 us
    dot_general x1, matrix products, shards(): jnp.einsum('ijkr,jlr->ikjl', scaled, lax.all_gather(form_strip, 'col', ax...  12.6 us
    another operation x1, local copies, waits for them, and re-layouts, shards(): flat.reshape(chans // nrow, nrow, nmom, ncol, width)  9.64 us
  transfers between devices with their start and end apart: 4, of which 4 were waited for; matrix products, arithmetic and copies ran while one was open for 4% of the time, Pallas kernels for 0%

commit v1 on v0

v1 whole, which is shorter than its diff:
```python
import jax
import jax.numpy as jnp
from jax import lax
from jax.sharding import PartitionSpec as P

ALL = ("row", "col")


def exchange(chunks):
    return lax.all_to_all(chunks, ALL, split_axis=0, concat_axis=0, tiled=True)


def mixing_weights(lam, coef, angular_coef, nlam):
    coef_table = (coef[..., None] == jnp.arange(angular_coef.shape[0], dtype=coef.dtype)).astype(jnp.float32)
    coef_value = jnp.sum(coef_table * angular_coef, axis=-1)
    lam_table = (lam[..., None] == jnp.arange(nlam, dtype=lam.dtype)).astype(jnp.float32)
    return jnp.sum(coef_value[..., None] * lam_table, axis=-2)


def weights_to_radial(mixing, kernels):
    chans, strips, nlam = mixing.shape
    radial = jnp.dot(mixing.reshape(chans * strips, nlam), kernels, precision=lax.Precision.HIGHEST)
    return radial.reshape(chans, strips, kernels.shape[1])


def shards(
    form_rows,
    form_strip,
    lam_index,
    coef_index,
    term_count,
    angular_coef,
    kernels,
    pivots,
    lower_inverse,
    panel,
):
    nrow = lax.axis_size("row")
    ncol = lax.axis_size("col")
    ndev = nrow * ncol
    row = lax.axis_index("row")
    col = lax.axis_index("col")
    me = row * ncol + col
    chans, nmom, nrad = form_rows.shape
    nstrip, terms = lam_index.shape[1:]
    nlam = kernels.shape[0]
    npiv = pivots.shape[0]
    scols = nstrip * nmom
    width = scols // ncol
    own = npiv // ndev
    group = chans // nrow
    bf16, f32 = jnp.bfloat16, jnp.float32

    position = lax.broadcasted_iota(jnp.int32, lam_index.shape, 2)
    lam = jnp.where(position < term_count[:, :, None], lam_index, nlam)
    at_row = pivots - me * (chans * nmom)
    row_pick = (at_row[:, None] == jnp.arange(chans * nmom, dtype=jnp.int32)).astype(bf16)
    picked = jnp.dot(row_pick, form_rows.reshape(chans * nmom, nrad), preferred_element_type=f32)
    at_chan = pivots // nmom - me * chans
    chan_pick = (at_chan[:, None] == jnp.arange(chans, dtype=jnp.int32)).astype(bf16)
    term_table = jnp.concatenate([lam.reshape(chans, -1), coef_index.reshape(chans, -1)], axis=1).astype(bf16)
    picked_terms = jnp.dot(chan_pick, term_table, preferred_element_type=f32)
    share = nmom // nrow
    strip_share = lax.dynamic_slice_in_dim(form_strip[0], row * share, share, axis=0)
    first = jnp.concatenate(
        [
            picked.astype(bf16).reshape(ndev, own * nrad),
            picked_terms.astype(bf16).reshape(ndev, own * 2 * nstrip * terms),
            jnp.broadcast_to(strip_share.reshape(1, -1), (ndev, share * nrad)),
        ],
        axis=1,
    )
    lanes = 128
    got = exchange(first.reshape(ndev, -1, lanes)).reshape(ndev, -1)
    cut1 = own * nrad
    cut2 = cut1 + own * 2 * nstrip * terms
    my_rows = jnp.sum(got[:, :cut1].astype(f32), axis=0).reshape(own, nrad)
    my_terms = jnp.sum(got[:, cut1:cut2].astype(f32), axis=0).reshape(own, 2, nstrip, terms)
    strip_all = got[:, cut2:].reshape(nrow, ncol, share, nrad).transpose(1, 0, 2, 3).reshape(nstrip, nmom, nrad)

    my_mixing = mixing_weights(my_terms[:, 0].astype(jnp.int32), my_terms[:, 1].astype(jnp.int32), angular_coef, nlam)
    my_radial = weights_to_radial(my_mixing, kernels)
    my_scaled = (my_rows[:, None, :] * my_radial).astype(bf16)
    my_chosen = jnp.einsum("ajr,jlr->ajl", my_scaled, strip_all, preferred_element_type=f32).astype(bf16)

    panel_cut = panel.reshape(panel.shape[0], ndev, -1).transpose(1, 0, 2)
    deep, wide = panel_cut.shape[1:]
    second = jnp.concatenate(
        [panel_cut, jnp.broadcast_to(my_chosen.reshape(1, -1, wide), (ndev, own * scols // wide, wide))], axis=1
    )
    got2 = exchange(second)

    mixing = mixing_weights(lam, coef_index, angular_coef, nlam)
    radial = weights_to_radial(mixing, kernels)
    scaled = (form_rows.astype(f32)[:, None] * radial[:, :, None, :]).astype(bf16)
    scaled = scaled.reshape(group, nrow, nstrip, nmom, nrad)
    blocks = jnp.einsum("qpjkr,jlr->pjlqk", scaled, strip_all, preferred_element_type=f32).astype(bf16)
    blocks = blocks.reshape(nrow, scols, group * nmom)

    chosen = got2[:, deep:].reshape(npiv, scols)
    low1 = lower_inverse.astype(bf16)
    rest = lower_inverse - low1.astype(f32)
    low2 = rest.astype(bf16)
    low3 = (rest - low2.astype(f32)).astype(bf16)
    upper = (
        jnp.dot(low1, chosen, preferred_element_type=f32)
        + (jnp.dot(low2, chosen, preferred_element_type=f32) + jnp.dot(low3, chosen, preferred_element_type=f32))
    ).astype(bf16)
    columns = got2[:, :deep].reshape(nrow, npiv, wide)
    update = jnp.einsum("tn,ptm->pnm", upper, columns, preferred_element_type=f32)
    done = (blocks.astype(f32) - update).astype(bf16).reshape(ndev, width, wide)
    final = exchange(done)
    trailing = final.transpose(1, 0, 2).reshape(width, ndev * wide).astype(f32)
    upper_t = lax.dynamic_slice_in_dim(upper, col * width, width, axis=1).T
    return (trailing, upper_t)


def solution(mesh):
    in_specs = (
        P(("row", "col"), None, None),
        P("col", None, None),
        P(("row", "col"), None, None),
        P(("row", "col"), None, None),
        P(("row", "col"), None),
        P(),
        P(),
        P(),
        P(),
        P("col", "row"),
    )
    out_specs = (P("col", "row"), P("col", None))
    return jax.shard_map(shards, mesh=mesh, in_specs=in_specs, out_specs=out_specs, check_vma=False)
```

time: 457 us -> 213 us (0.47)
  waiting for transfers between devices: 333 us -> 76.2 us
  starting transfers between devices: 9.75 us -> 27 us
  between operations: 13.9 us -> 1.06 us
  local copies, waits for them, and re-layouts: 54.5 us -> 63 us
  matrix products: 36.3 us -> 31.7 us
    all_gather x2 -> x0, waiting for transfers between devices: 235 us -> none  [the longest x1 199 us: shards(): lax.all_gather(panel, 'col', axis=0, tiled=True)]
    psum x1 -> x0, waiting for transfers between devices: 44.2 us -> none  [shards(): chosen_t = lax.psum(picked.astype(jnp.bfloat16), 'row').astype(jnp.float32)]
    convert_element_type x0 -> x5, local copies, waits for them, and re-layouts: none -> 43.2 us  [the longest x3 39.1 us: shards(): done = (blocks.astype(f32) - update).astype(bf16).reshape(ndev, width, wide)]
    all_to_all x1 -> x3, waiting for transfers between devices: 52 us -> 76.2 us  [exchange(): return lax.all_to_all(chunks, ALL, split_axis=0, concat_axis=0, tiled=True)]
    unnamed x12 -> x31, local copies, waits for them, and re-layouts: 30.7 us -> 9.88 us
    all_to_all x1 -> x3, starting transfers between devices: 9.45 us -> 27 us  [exchange(): return lax.all_to_all(chunks, ALL, split_axis=0, concat_axis=0, tiled=True)]
    another operation x1 -> x0, local copies, waits for them, and re-layouts: 9.64 us -> none  [shards(): flat.reshape(chans // nrow, nrow, nmom, ncol, width)]
    reshape x1 -> x6, local copies, waits for them, and re-layouts: 8.55 us -> 2.49 us  [the longest x1 1.79 us: shards(): chosen = got2[:, deep:].reshape(npiv, scols)]
  transfers between devices with their start and end apart: 4 -> 3, of which waited for: 4 -> 2; matrix products, arithmetic and copies ran while one was open for 4% -> 29% of each run, Pallas kernels for 0% -> 0%
where the time goes in v1:
time: 213 us; the launch traced here: 211 us
  waiting for transfers between devices  76.2 us (36%)
  local copies, waits for them, and re-layouts  63 us (30%)
  matrix products  31.7 us (15%)
  starting transfers between devices  27 us (13%)
  other arithmetic  12.3 us (6%)
    all_to_all x3, waiting for transfers between devices, exchange(): return lax.all_to_all(chunks, ALL, split_axis=0, concat_axis=0, tiled=True)  76.2 us
    convert_element_type x3, local copies, waits for them, and re-layouts, shards(): done = (blocks.astype(f32) - update).astype(bf16).reshape(ndev, width, wide)  39.1 us
    all_to_all x3, starting transfers between devices, exchange(): return lax.all_to_all(chunks, ALL, split_axis=0, concat_axis=0, tiled=True)  27 us
    dot_general x1, matrix products, shards(): jnp.einsum('qpjkr,jlr->pjlqk', scaled, strip_all, preferred_element_type=...  18.4 us
    unnamed x31, local copies, waits for them, and re-layouts  9.88 us
    dot_general x1, matrix products, shards(): jnp.einsum('tn,ptm->pnm', upper, columns, preferred_element_type=f32)  4.57 us
  transfers between devices with their start and end apart: 3, of which 2 were waited for; matrix products, arithmetic and copies ran while one was open for 29% of the time, Pallas kernels for 0%

profile of v1, /device:TPU:1, one launch (start us, length us, event | category | flops | bytes accessed | tf_op | source)
XLA Modules:
  0.0 211.4 jit_solution(7121948771823026650)
XLA Ops:
  0.7 0.9 convert_bitcast_fusion.2
  1.6 0.9 convert_bitcast_fusion.3
  2.6 0.7 broadcast_subtract_fusion
  3.3 0.3 convolution_convert_fusion
  3.5 0.2 reshape.105
  3.7 2.9 %fusion.7 = bf16[512,512]{1,0:T(8,128)(2,1)S(1)} fusion(bf16[2048,512]{1,0:T(8,128)(2,1)} %bitcast.109, s32[512]{0:T(512)S(1)} %get-tuple-element.6), kind=kOutput, calls=%fused_computation.18 | convolution fusion | flops 1075052544 | bytes 2623488 | tf_op jit(solution)/shard_map/dot_general | solution.py:58
  6.6 0.3 reshape.102
  7.0 0.4 maximum_bitcast_fusion
  7.4 1.6 copy.113
  9.0 11.9 %all-to-all-start = ((bf16[128,56,128]{2,1,0:T(8,128)(2,1)}), bf16[128,56,128]{2,1,0:T(8,128)(2,1)}, u32[]{:S(2)}, u32[]{:S(2)}) async-start(bf16[128,56,128]{2,1,0:T(8,128)(2,1)} %bitcast.32), calls=%async_computation | async-start | bytes 3670016 | tf_op jit(solution)/shard_map/all_to_all | solution.py:10
  20.9 2.1 copy.116
  23.0 24.6 %all-to-all-done = bf16[128,56,128]{2,1,0:T(8,128)(2,1)} async-done(((bf16[128,56,128]{2,1,0:T(8,128)(2,1)}), bf16[128,56,128]{2,1,0:T(8,128)(2,1)}, u32[]{:S(2)}, u32[]{:S(2)}) %all-to-all-start) | async-done | bytes 1835040 | tf_op jit(solution)/shard_map/all_to_all | solution.py:10
  47.5 1.9 copy.128
  49.6 0.1 convert_reduce_fusion
  49.7 0.4 copy.115
  50.2 0.3 select_reduce_fusion.3
  50.5 0.2 select_reduce_fusion.2
  50.7 0.2 fusion.8
  50.9 0.4 fusion.9
  51.3 0.1 broadcast_in_dim.15
  51.5 0.3 pad_maximum_fusion
  51.8 3.4 %copy.97 = bf16[128,48,256]{2,1,0:T(8,128)(2,1)} copy(bf16[128,48,256]{2,0,1:T(8,128)(2,1)S(1)} %pad_maximum_fusion) | data formatting | bytes 6291456 | tf_op jit(solution)/shard_map/concatenate | solution.py:88
  55.2 4.8 %all-to-all-start.1 = ((bf16[128,48,256]{2,1,0:T(8,128)(2,1)}), bf16[128,48,256]{2,1,0:T(8,128)(2,1)S(1)}, u32[]{:S(2)}, u32[]{:S(2)}) async-start(bf16[128,48,256]{2,1,0:T(8,128)(2,1)} %copy.97), calls=%async_computation.1 | async-start | bytes 6291456 | tf_op jit(solution)/shard_map/all_to_all | solution.py:10
  60.1 0.8 copy.90
  60.9 2.2 %select_reduce_fusion = f32[32,16,8]{2,1,0:T(8,128)S(1)} fusion(f32[64]{0:T(128)S(1)} %copy-done.9, s32[32,16,8]{2,1,0:T(8,128)} %copy.90), kind=kLoop, calls=%fused_computation.13 | loop fusion | flops 782336 | bytes 33024 | tf_op jit(solution)/shard_map/reduce_sum | solution.py:15
  63.1 0.2 copy.91
  63.3 0.8 select_reduce_fusion.1
  64.1 1.0 copy.109
  65.1 2.3 %convert.15 = f32[4,8,64,512]{3,2,1,0:T(8,128)S(1)} convert(bf16[4,8,64,512]{3,2,1,0:T(8,128)(2,1)} %bitcast.110) | non-fusion elementwise | flops 1048576 | bytes 6291456 | tf_op jit(solution)/shard_map/mul | solution.py:95
  67.4 1.0 fusion.20
  68.4 18.4 %convert_bitcast_fusion = f32[8,16,64,4,64]{4,2,0,3,1:T(8,128)} fusion(f32[4,8,16,512]{3,1,0,2:T(8,128)S(1)} %fusion.20, f32[4,8,64,512]{3,2,1,0:T(8,128)S(1)} %convert.15, bf16[8,16,8,512]{3,2,1,0:T(8,128)(2,1)S(1)} %bitcast.107), kind=kOutput, calls=%fused_computation.4 | convolution fusion | flops 2185232384 | bytes 14680064 | tf_op jit(solution)/shard_map/qpjkr,jlr->pjlqk/dot_general | solution.py:97
  86.8 18.2 %copy.94 = f32[8,16,64,4,64]{2,1,4,3,0:T(8,128)} copy(f32[8,16,64,4,64]{4,2,0,3,1:T(8,128)} %convert_bitcast_fusion) | data formatting | bytes 16777216 | tf_op jit(solution)/shard_map/convert_element_type | solution.py:111
  105.0 14.5 %reshape.116 = f32[8,1024,256]{1,2,0:T(8,128)} reshape(f32[8,16,64,4,64]{2,1,4,3,0:T(8,128)} %copy.94) | data formatting | bytes 16777216 | tf_op jit(solution)/shard_map/convert_element_type | solution.py:111
  119.4 1.6 copy-done.2
  121.1 1.1 slice.34
  122.1 1.8 reshape.113
  123.9 2.5 %fusion.17 = f32[512,1024]{0,1:T(8,128)S(1)} fusion(bf16[512,1024]{1,0:T(8,128)(2,1)S(1)} %reshape.113, f32[512,512]{1,0:T(8,128)} %param.18), kind=kOutput, calls=%fused_computation.37 | convolution fusion | flops 537919488 | bytes 4194304 | tf_op jit(solution)/shard_map/dot_general | solution.py:107
  126.4 0.8 fusion.19
  127.2 0.8 fusion.5
  128.0 1.4 slice-done.2
  129.4 0.9 slice-done
  130.3 4.6 %fusion.3 = bf16[8,1024,256]{1,2,0:T(8,128)(2,1)} fusion(f32[8,1024,256]{1,2,0:T(8,128)S(1)} %bitcast.100, bf16[8,512,256]{2,1,0:T(8,128)(2,1)S(1)} %bitcast.98, bf16[512,1024]{0,1:T(8,128)(2,1)S(1)} %fusion.5), kind=kOutput, calls=%fused_computation.6 | convolution fusion | flops 2151677952 | bytes 15728640 | tf_op jit(solution)/shard_map/tn,ptm->pnm/dot_general | solution.py:110
  134.8 6.5 %copy.102 = bf16[8,1024,256]{2,1,0:T(8,128)(2,1)} copy(bf16[8,1024,256]{1,2,0:T(8,128)(2,1)} %fusion.3) | data formatting | bytes 8388608 | tf_op jit(solution)/shard_map/convert_element_type | solution.py:111
  141.3 10.4 %all-to-all-start.2 = ((bf16[128,64,256]{2,1,0:T(8,128)(2,1)}), bf16[128,64,256]{2,1,0:T(8,128)(2,1)}, u32[]{:S(2)}, u32[]{:S(2)}) async-start(bf16[128,64,256]{2,1,0:T(8,128)(2,1)} %bitcast.97), calls=%async_computation.2 | async-start | bytes 8388608 | tf_op jit(solution)/shard_map/all_to_all | solution.py:10
  151.7 0.6 dynamic-slice_bitcast_fusion
  152.3 51.7 %all-to-all-done.2 = bf16[128,64,256]{2,1,0:T(8,128)(2,1)} async-done(((bf16[128,64,256]{2,1,0:T(8,128)(2,1)}), bf16[128,64,256]{2,1,0:T(8,128)(2,1)}, u32[]{:S(2)}, u32[]{:S(2)}) %all-to-all-start.2) | async-done | bytes 4194336 | tf_op jit(solution)/shard_map/all_to_all | solution.py:10
  204.0 3.3 %convert_bitcast_fusion.1 = f32[128,8,8,256]{3,2,1,0:T(8,128)S(1)} fusion(bf16[128,64,256]{2,1,0:T(8,128)(2,1)} %all-to-all-done.2), kind=kLoop, calls=%fused_computation.7 | loop fusion | flops 2097152 | bytes 12582912
  207.3 4.1 %copy.111 = f32[128,8,8,256]{3,2,0,1:T(8,128)} copy(f32[128,8,8,256]{3,2,1,0:T(8,128)S(1)} %convert_bitcast_fusion.1) | data formatting | bytes 16777216 | tf_op jit(solution)/shard_map/convert_element_type | solution.py:113
  (37 shorter events, 0.5 us)
Async XLA Ops:
  0.6 6.3 %copy-start = (bf16[1,64,512]{2,1,0:T(8,128)(2,1)S(1)}, bf16[1,64,512]{2,1,0:T(8,128)(2,1)}, u32[]{:S(2)}) copy-start(bf16[1,64,512]{2,1,0:T(8,128)(2,1)} %param.11) | copy-start | bytes 196612
  9.0 38.6 %all-to-all-start = ((bf16[128,56,128]{2,1,0:T(8,128)(2,1)}), bf16[128,56,128]{2,1,0:T(8,128)(2,1)}, u32[]{:S(2)}, u32[]{:S(2)}) async-start(bf16[128,56,128]{2,1,0:T(8,128)(2,1)} %bitcast.32), calls=%async_computation | async-start | bytes 3670016 | tf_op jit(solution)/shard_map/all_to_all | solution.py:10
  49.4 0.8 copy-start.9
  49.4 1.3 copy-start.7
  50.1 1.7 copy-start.4
  55.2 4.8 %copy-start.6 = (s32[32,16,8]{0,2,1:T(8,128)S(1)}, s32[32,16,8]{0,2,1:T(8,128)}, u32[]{:S(2)}) copy-start(s32[32,16,8]{0,2,1:T(8,128)} %param.13) | copy-start | bytes 49156
  55.2 64.2 %all-to-all-start.1 = ((bf16[128,48,256]{2,1,0:T(8,128)(2,1)}), bf16[128,48,256]{2,1,0:T(8,128)(2,1)S(1)}, u32[]{:S(2)}, u32[]{:S(2)}) async-start(bf16[128,48,256]{2,1,0:T(8,128)(2,1)} %copy.97), calls=%async_computation.1 | async-start | bytes 6291456 | tf_op jit(solution)/shard_map/all_to_all | solution.py:10
  65.1 2.3 %copy-start.8 = (f32[16,512]{1,0:T(8,128)S(1)}, f32[16,512]{1,0:T(8,128)}, u32[]{:S(2)}) copy-start(f32[16,512]{1,0:T(8,128)} %param.16) | copy-start | bytes 98308
  65.1 3.3 %copy-start.5 = (bf16[16,8,8,512]{3,2,1,0:T(8,128)(2,1)S(1)}, bf16[16,8,8,512]{3,2,1,0:T(8,128)(2,1)}, u32[]{:S(2)}) copy-start(bf16[16,8,8,512]{3,2,1,0:T(8,128)(2,1)} %copy-done.4) | copy-start | bytes 3145732
  119.4 1.6 copy-start.2
  122.1 4.3 %copy-start.3 = (f32[512,512]{1,0:T(8,128)S(1)}, f32[512,512]{1,0:T(8,128)}, u32[]{:S(2)}) copy-start(f32[512,512]{1,0:T(8,128)} %param.18) | copy-start | bytes 3145732
  123.9 4.1 %slice-start.1 = ((s8[8388608]{0:T(1024)(128)(4,1)}), s8[4194304]{0:T(1024)(128)(4,1)S(1)}, s32[]{:S(2)}) async-start(s8[8388608]{0:T(1024)(128)(4,1)} %bitcast.99), calls=%async_computation.4 | async-start | bytes 8388608
  127.2 2.2 %slice-start.2 = ((s8[8388608]{0:T(1024)(128)(4,1)}), s8[4194304]{0:T(1024)(128)(4,1)S(1)}, s32[]{:S(2)}) async-start(s8[8388608]{0:T(1024)(128)(4,1)} %bitcast.99), calls=%async_computation.5 | async-start | bytes 8388608
  128.0 2.3 %slice-start = ((bf16[128,48,256]{2,1,0:T(8,128)(2,1)}), bf16[128,32,256]{2,1,0:T(8,128)(2,1)S(1)}, s32[]{:S(2)}) async-start(bf16[128,48,256]{2,1,0:T(8,128)(2,1)} %copy-done.2), calls=%async_computation.3 | async-start | bytes 4194304 | tf_op jit(solution)/shard_map/slice | solution.py:109
  141.3 62.7 %all-to-all-start.2 = ((bf16[128,64,256]{2,1,0:T(8,128)(2,1)}), bf16[128,64,256]{2,1,0:T(8,128)(2,1)}, u32[]{:S(2)}, u32[]{:S(2)}) async-start(bf16[128,64,256]{2,1,0:T(8,128)(2,1)} %bitcast.97), calls=%async_computation.2 | async-start | bytes 8388608 | tf_op jit(solution)/shard_map/all_to_all | solution.py:10
  207.3 4.1 %copy-start.1 = (bf16[1,64,512]{2,1,0:T(8,128)(2,1)S(1)}, bf16[1,64,512]{2,1,0:T(8,128)(2,1)}, u32[]{:S(2)}) copy-start(bf16[1,64,512]{2,1,0:T(8,128)(2,1)} %param.11) | copy-start | bytes 196612

commit v2 on v1

v2 whole, which is shorter than its diff:
```python
import functools

import jax
import jax.numpy as jnp
from jax import lax
from jax.experimental import pallas as pl
from jax.experimental.pallas import tpu as pltpu
from jax.sharding import PartitionSpec as P

ALL = ("row", "col")
LANES = 128
BF16, F32 = jnp.bfloat16, jnp.float32
NT = (((1,), (1,)), ((), ()))


def room(mebibytes):
    return pltpu.CompilerParams(vmem_limit_bytes=mebibytes * 1024 * 1024)


def exchange(chunks):
    return lax.all_to_all(chunks, ALL, split_axis=0, concat_axis=0, tiled=True)


def cost(flops, bytes_accessed):
    return pl.CostEstimate(flops=flops, bytes_accessed=bytes_accessed, transcendentals=0)


def mixing_weights(lam, coef, angular_coef, nlam):
    coef_table = (coef[..., None] == jnp.arange(angular_coef.shape[0], dtype=coef.dtype)).astype(F32)
    coef_value = jnp.sum(coef_table * angular_coef, axis=-1)
    lam_table = (lam[..., None] == jnp.arange(nlam, dtype=lam.dtype)).astype(F32)
    return jnp.sum(coef_value[..., None] * lam_table, axis=-2)


def weights_to_radial(mixing, kernels):
    chans, strips, nlam = mixing.shape
    radial = jnp.dot(mixing.reshape(chans * strips, nlam), kernels, precision=lax.Precision.HIGHEST)
    return radial.reshape(chans, strips, kernels.shape[1])


def pick_kernel(
    own,
    pivots_at,
    lam_at,
    coef_at,
    count_at,
    rows,
    form_strip_at,
    out,
    pivots,
    lam,
    coef,
    count,
    form_strip,
    acc,
    pieces,
    chunks,
    small,
    sems,
    done,
):
    pairs = ((form_strip_at, form_strip), (pivots_at, pivots), (lam_at, lam), (coef_at, coef), (count_at, count))
    loads = [pltpu.make_async_copy(source, target, small.at[i]) for i, (source, target) in enumerate(pairs)]
    for load in loads:
        load.start()
    npiv = pivots.shape[1]
    local, nrad = rows.shape
    nstrip, chans = count.shape
    terms = lam.shape[0] // nstrip
    nmom = local // chans
    steps = sems.shape[0]
    depth = local // steps
    ndev, deep1, _ = out.shape
    copies = [
        pltpu.make_async_copy(rows.at[pl.ds(s * depth, depth), :], pieces.at[s], sems.at[s]) for s in range(steps)
    ]
    for copy in copies:
        copy.start()
    row = lax.axis_index("row")
    me = row * lax.axis_size("col") + lax.axis_index("col")
    for load in loads:
        load.wait()
    tall = deep1 - own * acc.shape[1] // LANES
    halves = nmom // tall
    half, part = lax.rem(row, halves), lax.div(row, halves)
    share = form_strip[
        0,
        pl.ds(pl.multiple_of(half * tall, tall), tall),
        pl.ds(pl.multiple_of(part * LANES, LANES), LANES),
    ]
    chunks[:, :tall, :] = jnp.broadcast_to(share[None], (ndev, tall, LANES))
    column = jnp.broadcast_to(pivots[...].astype(F32), (LANES, npiv)).T[:, :1].astype(jnp.int32) - me * local
    counts = jnp.broadcast_to(count[...][:, None, :], (nstrip, terms, chans)).reshape(nstrip * terms, chans)
    position = lax.rem(lax.broadcasted_iota(jnp.int32, (nstrip * terms, chans), 0), terms)
    order = jnp.where(position < counts, lam[...], LANES)
    table = jnp.concatenate([order, coef[...]], axis=0).astype(F32).astype(BF16)
    first = lax.broadcasted_iota(jnp.int32, (npiv, chans), 1) * nmom
    pick = jnp.logical_and(column >= first, column < first + nmom).astype(F32).astype(BF16)
    acc[:, nrad:] = lax.dot_general(pick, table, NT, preferred_element_type=F32)
    total = None
    for s in range(steps):
        pick = (column - s * depth == lax.broadcasted_iota(jnp.int32, (npiv, depth), 1)).astype(F32).astype(BF16)
        copies[s].wait()
        part = jnp.dot(pick, pieces[s], preferred_element_type=F32)
        total = part if total is None else total + part
    acc[:, :nrad] = total
    groups = done.shape[0]
    per = ndev // groups
    low = lax.broadcasted_iota(jnp.int32, (per // 2, 2 * own, LANES), 1) < own
    sends = []
    for g in range(groups):
        tiles = []
        for at in range(0, acc.shape[1], 2 * LANES):
            left = acc[g * per * own : (g + 1) * per * own, at : at + LANES].reshape(per // 2, 2 * own, LANES)
            right = acc[g * per * own : (g + 1) * per * own, at + LANES : at + 2 * LANES].reshape(
                per // 2, 2 * own, LANES
            )
            even = jnp.where(low, left, pltpu.roll(right, own, 1))
            odd = jnp.where(low, pltpu.roll(left, own, 1), right)
            tiles.append(jnp.stack([even, odd], axis=1).reshape(per, 2 * own, LANES))
        chunks[g * per : (g + 1) * per, tall:, :] = jnp.concatenate(tiles, axis=1).astype(BF16)
        send = pltpu.make_async_copy(chunks.at[pl.ds(g * per, per)], out.at[pl.ds(g * per, per)], done.at[g])
        send.start()
        sends.append(send)
    for send in sends:
        send.wait()


def strip_copies(got, strip, sems):
    nstrip, nmom, nrad = strip.shape
    nrow = got.shape[0] // nstrip
    halves = nrow * LANES // nrad
    tall = nmom // halves
    return [
        pltpu.make_async_copy(
            got.at[pl.ds(row * nstrip, nstrip), pl.ds(0, tall), :],
            strip.at[:, pl.ds(row % halves * tall, tall), pl.ds(row // halves * LANES, LANES)],
            sems.at[row],
        )
        for row in range(nrow)
    ]


def chosen_kernel(
    own, got, kernels_at, angular_at, kept, second, mail, kernels, angular, strip, wave, loads, sent
):
    del kept
    nstrip, nmom, nrad = strip.shape
    ndev, deep1, _ = got.shape
    nrow = ndev // nstrip
    parts = nrad // LANES
    halves = nrow // parts
    tall = nmom // halves
    first = [
        pltpu.make_async_copy(got.at[:, pl.ds(tall, deep1 - tall), :], mail, loads.at[nrow]),
        pltpu.make_async_copy(kernels_at, kernels, loads.at[nrow + 1]),
        pltpu.make_async_copy(angular_at, angular, loads.at[nrow + 2]),
    ]
    later = strip_copies(got, strip, loads)
    for copy in first + later:
        copy.start()
    for copy in first:
        copy.wait()
    mine = jnp.sum(mail[...].astype(F32), axis=0)
    nlam = kernels.shape[0]
    ncoef = angular.shape[0]
    terms = LANES // nstrip
    diagonal = (
        lax.broadcasted_iota(jnp.int32, (nstrip, LANES), 0)
        == lax.broadcasted_iota(jnp.int32, (nstrip, LANES), 1) // terms
    )
    coefs = lax.broadcasted_iota(jnp.int32, (ncoef, LANES), 0).astype(F32)
    lams = lax.broadcasted_iota(jnp.int32, (nlam, LANES), 0).astype(F32)
    lefts, rights, forms = [], [], []
    for a in range(own):
        lam = mine[parts * own + a : parts * own + a + 1, :]
        coef = mine[(parts + 1) * own + a : (parts + 1) * own + a + 1, :]
        value = jnp.sum(jnp.where(coef == coefs, angular[...], 0.0), axis=0, keepdims=True)
        left = jnp.where(diagonal, value, 0.0)
        lefts.append(
            jnp.concatenate([left if b == a else jnp.zeros_like(left) for b in range(own)], axis=1)
        )
        rights.append((lam == lams).astype(F32))
        form = jnp.concatenate([mine[g * own + a : g * own + a + 1, :] for g in range(parts)], axis=1)
        forms.append(jnp.broadcast_to(form, (nstrip, nrad)))
    mixing = lax.dot_general(
        jnp.concatenate(lefts, axis=0),
        jnp.concatenate(rights, axis=1),
        NT,
        precision=lax.Precision.HIGHEST,
        preferred_element_type=F32,
    )
    radial = jnp.dot(mixing, kernels[...], precision=lax.Precision.HIGHEST, preferred_element_type=F32)
    scaled = (jnp.concatenate(forms, axis=0) * radial).astype(BF16)
    scols = nstrip * nmom
    for copy in later:
        copy.wait()
    full = lax.dot_general(scaled, strip[...].reshape(scols, nrad), NT, preferred_element_type=F32)
    keep = (
        lax.broadcasted_iota(jnp.int32, (nstrip, scols), 0)
        == lax.broadcasted_iota(jnp.int32, (nstrip, scols), 1) // nmom
    )
    chosen = [
        jnp.sum(jnp.where(keep, full[a * nstrip : (a + 1) * nstrip], 0.0), axis=0, keepdims=True) for a in range(own)
    ]
    chosen = jnp.concatenate(chosen, axis=0)
    many, rows, wide = wave.shape
    tile = jnp.concatenate([chosen[:, at : at + wide] for at in range(0, scols, wide)], axis=0).astype(BF16)
    wave[...] = jnp.broadcast_to(tile[None], wave.shape)
    sends = []
    for g in range(ndev // many):
        send = pltpu.make_async_copy(
            wave, second.at[pl.ds(g * many, many), pl.ds(second.shape[1] - rows, rows), :], sent.at[g]
        )
        send.start()
        sends.append(send)
    for send in sends:
        send.wait()


def assemble_kernel(rows, radial, got, out, strip, sems):
    group, nrow, nmom, nrad = rows.shape
    nstrip = strip.shape[0]
    copies = strip_copies(got, strip, sems)
    for copy in copies:
        copy.start()
    for copy in copies:
        copy.wait()

    def one(p, carry):
        forms = [rows[q, p].astype(F32) for q in range(group)]
        for j in range(nstrip):
            scaled = jnp.concatenate(
                [(forms[q] * radial[q, p, j : j + 1, :]).astype(BF16) for q in range(group)], axis=0
            )
            block = lax.dot_general(strip[j], scaled, NT, preferred_element_type=F32)
            out[p, j * nmom : (j + 1) * nmom, :] = block.astype(BF16)
        return carry

    lax.fori_loop(0, nrow, one, 0)


def update_kernel(
    own, got, lower, blocks, out, upper_t, waves, low, columns, before, upper_all, spread, chosen, results, sems, sent
):
    npiv, scols = chosen.shape
    ndev, rows, wide = waves.shape
    nrow, ncol, deep, _ = columns.shape
    wave = pltpu.make_async_copy(got.at[:, pl.ds(deep, rows), :], waves, sems.at[2 * nrow])
    wave.start()
    bottom = pltpu.make_async_copy(lower, low, sems.at[2 * nrow + 1])
    bottom.start()
    loads = []
    for p in range(nrow):
        load = (
            pltpu.make_async_copy(got.at[pl.ds(p * ncol, ncol), pl.ds(0, deep), :], columns.at[p], sems.at[p]),
            pltpu.make_async_copy(blocks.at[p], before.at[p], sems.at[nrow + p]),
        )
        for copy in load:
            copy.start()
        loads.append(load)
    wave.wait()
    for b in range(wide // LANES):
        spread[b] = waves[:, :, b * LANES : (b + 1) * LANES].astype(F32).reshape(ndev * rows, LANES)
        for h in range(scols // wide):
            start = h * wide + b * LANES
            for a in range(own):
                chosen[a * ndev : (a + 1) * ndev, start : start + LANES] = spread[
                    b, pl.ds(h * own + a, ndev, stride=rows), :
                ].astype(BF16)
    bottom.wait()
    low1 = low[...].astype(BF16)
    low2 = (low[...] - low1.astype(F32)).astype(BF16)
    for at in range(0, scols, wide):
        rows_of = chosen[:, at : at + wide]
        upper = jnp.dot(low1, rows_of, preferred_element_type=F32) + jnp.dot(
            low2, rows_of, preferred_element_type=F32
        )
        upper_all[at : at + wide, :] = upper.T.astype(BF16)
    width = upper_t.shape[0]
    upper_t[...] = upper_all[pl.ds(pl.multiple_of(lax.axis_index("col") * width, width), width), :]
    for load in loads:
        for copy in load:
            copy.wait()
    sends = []
    for p in range(nrow):
        change = jnp.dot(upper_all[...], columns[p].reshape(npiv, wide), preferred_element_type=F32)
        results[p] = (before[p].astype(F32) - change).astype(BF16)
        send = pltpu.make_async_copy(results.at[p], out.at[p], sent.at[p])
        send.start()
        sends.append(send)
    for send in sends:
        send.wait()


def widen_kernel(got, out, broad, sent):
    ndev, width, wide = got.shape
    steps = sent.shape[0]
    many = ndev // steps
    sends = []
    for s in range(steps):
        for b in range(s * many, (s + 1) * many):
            broad[:, b * wide : (b + 1) * wide] = got[b].astype(F32)
        span = pl.ds(s * many * wide, many * wide)
        send = pltpu.make_async_copy(broad.at[:, span], out.at[:, span], sent.at[s])
        send.start()
        sends.append(send)
    for send in sends:
        send.wait()


def shards(
    form_rows,
    form_strip,
    lam_index,
    coef_index,
    term_count,
    angular_coef,
    kernels,
    pivots,
    lower_inverse,
    panel,
):
    nrow = lax.axis_size("row")
    ncol = lax.axis_size("col")
    ndev = nrow * ncol
    chans, nmom, nrad = form_rows.shape
    nstrip, terms = lam_index.shape[1:]
    nlam = kernels.shape[0]
    npiv = pivots.shape[0]
    scols = nstrip * nmom
    width = scols // ncol
    own = npiv // ndev
    group = chans // nrow
    local = chans * nmom
    vmem = pl.BlockSpec(memory_space=pltpu.VMEM)
    anywhere = pl.BlockSpec(memory_space=pl.ANY)
    dma = pltpu.SemaphoreType.DMA

    parts = nrad // LANES
    halves = nrow // parts
    tall = nmom // halves
    extra = 2 * nstrip * terms
    deep1 = tall + own * (nrad + extra) // LANES
    steps, groups = 4, 4
    first = pl.pallas_call(
        functools.partial(pick_kernel, own),
        out_shape=jax.ShapeDtypeStruct((ndev, deep1, LANES), BF16),
        in_specs=[anywhere] * 6,
        out_specs=anywhere,
        scratch_shapes=[
            pltpu.VMEM((1, npiv), jnp.int32),
            pltpu.VMEM((nstrip * terms, chans), jnp.int32),
            pltpu.VMEM((nstrip * terms, chans), jnp.int32),
            pltpu.VMEM((nstrip, chans), jnp.int32),
            pltpu.VMEM(form_strip.shape, BF16),
            pltpu.VMEM((npiv, nrad + extra), F32),
            pltpu.VMEM((steps, local // steps, nrad), BF16),
            pltpu.VMEM((ndev, deep1, LANES), BF16),
            dma((5,)),
            dma((steps,)),
            dma((groups,)),
        ],
        compiler_params=room(56),
        cost_estimate=cost(2 * npiv * local * nrad, 4 << 20),
        name="pick_pivots",
    )(
        pivots[None, :],
        lam_index.transpose(1, 2, 0).reshape(nstrip * terms, chans),
        coef_index.transpose(1, 2, 0).reshape(nstrip * terms, chans),
        term_count.T,
        form_rows.reshape(local, nrad),
        form_strip,
    )
    got = exchange(first)

    deep, wide = panel.shape[0], panel.shape[1] // ndev
    cut = panel.reshape(deep, ndev, wide).transpose(1, 0, 2)
    wave_rows = own * scols // wide
    second = jnp.pad(cut, ((0, 0), (0, wave_rows), (0, 0)))
    many = 32
    second = pl.pallas_call(
        functools.partial(chosen_kernel, own),
        out_shape=jax.ShapeDtypeStruct(second.shape, BF16),
        in_specs=[anywhere] * 4,
        out_specs=anywhere,
        scratch_shapes=[
            pltpu.VMEM((ndev, deep1 - tall, LANES), BF16),
            pltpu.VMEM(kernels.shape, F32),
            pltpu.VMEM((angular_coef.shape[0], 1), F32),
            pltpu.VMEM((nstrip, nmom, nrad), BF16),
            pltpu.VMEM((many, wave_rows, wide), BF16),
            dma((nrow + 3,)),
            dma((ndev // many,)),
        ],
        input_output_aliases={3: 0},
        compiler_params=room(61),
        cost_estimate=cost(2 * own * nstrip * scols * nrad, 4 << 20),
        name="chosen_rows",
    )(got, kernels, angular_coef[:, None], second)
    got2 = exchange(second)

    position = lax.broadcasted_iota(jnp.int32, lam_index.shape, 2)
    lam = jnp.where(position < term_count[:, :, None], lam_index, nlam)
    mixing = mixing_weights(lam, coef_index, angular_coef, nlam)
    radial = weights_to_radial(mixing, kernels)
    blocks = pl.pallas_call(
        assemble_kernel,
        out_shape=jax.ShapeDtypeStruct((nrow, scols, group * nmom), BF16),
        in_specs=[vmem, vmem, anywhere],
        out_specs=vmem,
        scratch_shapes=[pltpu.VMEM((nstrip, nmom, nrad), BF16), dma((nrow,))],
        compiler_params=room(56),
        cost_estimate=cost(2 * local * scols * nrad * 4, 8 << 20),
        name="assemble_strip",
    )(form_rows.reshape(group, nrow, nmom, nrad), radial.reshape(group, nrow, nstrip, nrad), got)

    lower = lower_inverse.reshape(npiv, ndev, own).transpose(0, 2, 1).reshape(npiv, npiv)
    done, upper_t = pl.pallas_call(
        functools.partial(update_kernel, own),
        out_shape=(
            jax.ShapeDtypeStruct((nrow, scols, wide), BF16),
            jax.ShapeDtypeStruct((width, npiv), BF16),
        ),
        in_specs=[anywhere, anywhere, anywhere],
        out_specs=(anywhere, vmem),
        scratch_shapes=[
            pltpu.VMEM((ndev, wave_rows, wide), BF16),
            pltpu.VMEM((npiv, npiv), F32),
            pltpu.VMEM((nrow, ncol, deep, wide), BF16),
            pltpu.VMEM((nrow, scols, wide), BF16),
            pltpu.VMEM((scols, npiv), BF16),
            pltpu.VMEM((wide // LANES, ndev * wave_rows, LANES), F32),
            pltpu.VMEM((npiv, scols), BF16),
            pltpu.VMEM((nrow, scols, wide), BF16),
            dma((2 * nrow + 2,)),
            dma((nrow,)),
        ],
        compiler_params=room(56),
        cost_estimate=cost(2 * npiv * scols * (3 * npiv + local), 12 << 20),
        name="update_blocks",
    )(got2, lower, blocks)
    final = exchange(done.reshape(ndev, width, wide))
    steps = 16
    trailing = pl.pallas_call(
        widen_kernel,
        out_shape=jax.ShapeDtypeStruct((width, ndev * wide), F32),
        in_specs=[vmem],
        out_specs=anywhere,
        scratch_shapes=[pltpu.VMEM((width, ndev * wide), F32), dma((steps,))],
        compiler_params=room(20),
        cost_estimate=cost(ndev * width * wide, 12 << 20),
        name="widen_blocks",
    )(final)
    return (trailing, upper_t)


def solution(mesh):
    in_specs = (
        P(("row", "col"), None, None),
        P("col", None, None),
        P(("row", "col"), None, None),
        P(("row", "col"), None, None),
        P(("row", "col"), None),
        P(),
        P(),
        P(),
        P(),
        P("col", "row"),
    )
    out_specs = (P("col", "row"), P("col", None))
    return jax.shard_map(shards, mesh=mesh, in_specs=in_specs, out_specs=out_specs, check_vma=False)
```

time: 213 us -> 164 us (0.77)
  blocking collectives: 0 us -> 57.2 us
  local copies, waits for them, and re-layouts: 63 us -> 8.54 us
  Pallas kernels: 0 us -> 35.6 us
  waiting for transfers between devices: 76.2 us -> 40.8 us
  matrix products: 31.7 us -> 1.96 us
  other arithmetic: 12.3 us -> 1.49 us
  starting transfers between devices: 27 us -> 17.3 us
    all_to_all x0 -> x1, blocking collectives: none -> 57.2 us  [exchange(): return lax.all_to_all(chunks, ALL, split_axis=0, concat_axis=0, tiled=True)]
    convert_element_type x5 -> x0, local copies, waits for them, and re-layouts: 43.2 us -> none  [the longest x3 39.1 us: shards(): done = (blocks.astype(f32) - update).astype(bf16).reshape(ndev, width, wide)]
    pallas_call x0 -> x5, Pallas kernels: none -> 35.6 us  [the longest x1 16.3 us: shards(): pl.pallas_call(assemble_kernel, out_shape=jax.ShapeDtypeStruct((nrow, sco...]
    all_to_all x3 -> x2, waiting for transfers between devices: 76.2 us -> 40.8 us  [exchange(): return lax.all_to_all(chunks, ALL, split_axis=0, concat_axis=0, tiled=True)]
    dot_general x8 -> x0, matrix products: 30.5 us -> none  [the longest x1 18.4 us: shards(): jnp.einsum('qpjkr,jlr->pjlqk', scaled, strip_all, preferred_element_type=...]
    all_to_all x3 -> x2, starting transfers between devices: 27 us -> 17.3 us  [exchange(): return lax.all_to_all(chunks, ALL, split_axis=0, concat_axis=0, tiled=True)]
    unnamed x31 -> x17, local copies, waits for them, and re-layouts: 9.88 us -> 2.87 us
    unnamed x3 -> x0, other arithmetic: 3.67 us -> none
  transfers between devices with their start and end apart: 3 -> 2, of which waited for: 2 -> 2; matrix products, arithmetic and copies ran while one was open for 29% -> 6% of each run, Pallas kernels for 0% -> 10%
where the time goes in v2:
time: 164 us
  blocking collectives  57.2 us (35%)
  waiting for transfers between devices  40.8 us (25%)
  Pallas kernels  35.6 us (22%)
  starting transfers between devices  17.3 us (11%)
  local copies, waits for them, and re-layouts  8.54 us (5%)
  matrix products  1.96 us (1%)
    all_to_all x1, blocking collectives, exchange(): return lax.all_to_all(chunks, ALL, split_axis=0, concat_axis=0, tiled=True)  57.2 us
    all_to_all x2, waiting for transfers between devices, exchange(): return lax.all_to_all(chunks, ALL, split_axis=0, concat_axis=0, tiled=True)  40.8 us
    all_to_all x2, starting transfers between devices, exchange(): return lax.all_to_all(chunks, ALL, split_axis=0, concat_axis=0, tiled=True)  17.3 us
    pallas_call x1, Pallas kernels, shards(): pl.pallas_call(assemble_kernel, out_shape=jax.ShapeDtypeStruct((nrow, sco...  16.3 us
    pallas_call x1, Pallas kernels, shards(): pl.pallas_call(functools.partial(update_kernel, own), out_shape=(jax.Shap...  7.74 us
    pallas_call x1, Pallas kernels, shards(): pl.pallas_call(functools.partial(pick_kernel, own), out_shape=jax.ShapeDt...  4.57 us
    pallas_call x1, Pallas kernels, shards(): pl.pallas_call(functools.partial(chosen_kernel, own), out_shape=jax.Shape...  3.58 us
    pallas_call x1, Pallas kernels, shards(): pl.pallas_call(widen_kernel, out_shape=jax.ShapeDtypeStruct((width, ndev...  3.45 us
  transfers between devices with their start and end apart: 2, of which 2 were waited for; matrix products, arithmetic and copies ran while one was open for 6% of the time, Pallas kernels for 10%

profile of v2, /device:TPU:1, one launch (start us, length us, event | category | flops | bytes accessed | tf_op | source)
XLA Modules:
  0.0 163.7 jit_solution(2134123105394790518)
XLA Ops:
  0.6 4.6 %pick_pivots.1 = bf16[128,56,128]{2,1,0:T(8,128)(2,1)} custom-call(s32[1,512]{1,0:T(1,128)} %bitcast.45, s32[128,32]{1,0:T(8,128)} %bitcast.43, s32[128,32]{1,0:T(8,128)} %bitcast.42, s32[16,32]{1,0:T(8,128)} %bitcast.44, bf16[2048,512]{1,0:T(8,128)(2,1)} %bitcast.37, bf16[1,64,512]{2,1,0:T(8,128)(2,1)} %form_strip_at.1), custom_call_target="tpu_custom_call" | custom-call | flops 1073741824 | bytes 4194304 | tf_op jit(solution)/shard_map/pick_pivots/pallas_call | solution.py:346
  5.2 0.0 copy-start.6
  5.2 11.5 %all-to-all-start = ((bf16[128,56,128]{2,1,0:T(8,128)(2,1)}), bf16[128,56,128]{2,1,0:T(8,128)(2,1)S(1)}, u32[]{:S(2)}, u32[]{:S(2)}) async-start(bf16[128,56,128]{2,1,0:T(8,128)(2,1)} %pick_pivots.1), calls=%async_computation | async-start | bytes 3670016 | tf_op jit(solution)/shard_map/all_to_all | solution.py:21
  16.7 0.0 copy-done.6
  16.7 0.7 copy.31.angular_at
  17.5 1.9 %copy.42 = bf16[4,128,8,256]{3,2,0,1:T(8,128)(2,1)S(1)} copy(bf16[4,128,8,256]{3,2,1,0:T(8,128)(2,1)} %bitcast.39) | data formatting | bytes 4194304 | tf_op jit(solution)/shard_map/reshape | solution.py:378
  19.3 1.9 %pad.4.kept = bf16[128,48,256]{2,1,0:T(8,128)(2,1)} pad(bf16[128,32,256]{2,1,0:T(8,128)(2,1)S(1)} %bitcast.33, bf16[]{:T(256)} %constant.6.clone.1), padding=0_0x0_16x0_0 | pad | bytes 5242882 | tf_op jit(solution)/shard_map/jit(_pad)/pad | solution.py:380
  21.2 22.5 %all-to-all-done.got = bf16[128,56,128]{2,1,0:T(8,128)(2,1)S(1)} async-done(((bf16[128,56,128]{2,1,0:T(8,128)(2,1)}), bf16[128,56,128]{2,1,0:T(8,128)(2,1)S(1)}, u32[]{:S(2)}, u32[]{:S(2)}) %all-to-all-start) | async-done | bytes 1835040 | tf_op jit(solution)/shard_map/all_to_all | solution.py:21
  43.7 0.0 copy-start
  43.7 1.3 copy-done
  45.0 3.6 %chosen_rows.1 = bf16[128,48,256]{2,1,0:T(8,128)(2,1)} custom-call(bf16[128,56,128]{2,1,0:T(8,128)(2,1)} %copy-done, f32[16,512]{1,0:T(8,128)} %kernels_at.1, f32[64,1]{1,0:T(8,128)} %copy.31.angular_at, bf16[128,48,256]{2,1,0:T(8,128)(2,1)} %pad.4.kept), custom_call_target="tpu_custom_call", output_to_operand_aliasing={{}: (3, {})} | custom-call | flops 67108864 | bytes 4194304 | tf_op jit(solution)/shard_map/chosen_rows/pallas_call | solution.py:382
  48.6 0.0 copy-start.2
  48.6 0.0 copy-start.3
  48.6 0.0 copy-start.5
  48.6 5.8 %all-to-all-start.1 = ((bf16[128,48,256]{2,1,0:T(8,128)(2,1)}), bf16[128,48,256]{2,1,0:T(8,128)(2,1)}, u32[]{:S(2)}, u32[]{:S(2)}) async-start(bf16[128,48,256]{2,1,0:T(8,128)(2,1)} %chosen_rows.1), calls=%async_computation.1 | async-start | bytes 6291456 | tf_op jit(solution)/shard_map/all_to_all | solution.py:21
  54.4 0.0 copy-done.2
  54.5 0.0 copy-start.1
  54.5 0.2 copy.34
  54.6 1.3 select_reduce_fusion
  56.0 0.2 copy.35
  56.1 0.0 copy-done.3
  56.1 0.0 copy-done.5
  56.2 0.1 select_reduce_fusion.1
  56.3 0.2 copy.36
  56.5 0.0 copy-done.1
  56.5 0.3 copy.32
  56.8 0.3 reshape.40
  57.1 0.0 copy-start.4
  57.2 0.6 copy.33
  57.7 1.0 copy.43
  58.8 0.0 copy-done.4
  58.8 2.0 %fusion.1.radial = f32[4,8,16,512]{3,2,1,0:T(8,128)} fusion(f32[4,8,16,16]{3,2,1,0:T(8,128)S(1)} %bitcast.41, f32[16,512]{1,0:T(8,128)S(1)} %copy-done.4), kind=kOutput, calls=%fused_computation.8 | convolution fusion | flops 50331648 | bytes 1114112 | tf_op jit(solution)/shard_map/dot_general | solution.py:37
  60.7 16.3 %assemble_strip.1.blocks = bf16[8,1024,256]{2,1,0:T(8,128)(2,1)} custom-call(bf16[4,8,64,512]{3,2,1,0:T(8,128)(2,1)} %bitcast.38, f32[4,8,16,512]{3,2,1,0:T(8,128)} %fusion.1.radial, bf16[128,56,128]{2,1,0:T(8,128)(2,1)} %copy-done), custom_call_target="tpu_custom_call" | custom-call | flops 8589934592 | bytes 8388608 | tf_op jit(solution)/shard_map/assemble_strip/pallas_call | solution.py:407
  77.0 18.3 %all-to-all-done.1.got = bf16[128,48,256]{2,1,0:T(8,128)(2,1)} async-done(((bf16[128,48,256]{2,1,0:T(8,128)(2,1)}), bf16[128,48,256]{2,1,0:T(8,128)(2,1)}, u32[]{:S(2)}, u32[]{:S(2)}) %all-to-all-start.1) | async-done | bytes 3145760 | tf_op jit(solution)/shard_map/all_to_all | solution.py:21
  95.3 7.7 %update_blocks.1 = (bf16[8,1024,256]{2,1,0:T(8,128)(2,1)}, bf16[64,512]{1,0:T(8,128)(2,1)}) custom-call(bf16[128,48,256]{2,1,0:T(8,128)(2,1)} %all-to-all-done.1.got, f32[512,512]{1,0:T(8,128)} %bitcast.40, bf16[8,1024,256]{2,1,0:T(8,128)(2,1)} %assemble_strip.1.blocks), custom_call_target="tpu_custom_call" | custom-call | flops 3758096384 | bytes 12582912 | tf_op jit(solution)/shard_map/update_blocks/pallas_call | solution.py:419
  103.1 57.2 %all_to_all.15.got = bf16[128,64,256]{2,1,0:T(8,128)(2,1)S(1)} all-to-all(bf16[128,64,256]{2,1,0:T(8,128)(2,1)} %bitcast.34), channel_id=1, replica_groups=mesh['row'=8,'col'=16] {'row','col'}, dimensions={0} | all-to-all | bytes 8388608 | tf_op jit(solution)/shard_map/all_to_all | solution.py:21
  160.2 3.4 %widen_blocks.1 = f32[64,32768]{1,0:T(8,128)} custom-call(bf16[128,64,256]{2,1,0:T(8,128)(2,1)S(1)} %all_to_all.15.got), custom_call_target="tpu_custom_call" | custom-call | flops 2097152 | bytes 12582912 | tf_op jit(solution)/shard_map/widen_blocks/pallas_call | solution.py:445
  (1 shorter events, 0.0 us)
Async XLA Ops:
  5.2 11.5 %copy-start.6 = (f32[64]{0:T(128)S(1)}, f32[64]{0:T(128)}, u32[]{:S(2)}) copy-start(f32[64]{0:T(128)} %param.15) | copy-start | bytes 772
  5.2 38.5 %all-to-all-start = ((bf16[128,56,128]{2,1,0:T(8,128)(2,1)}), bf16[128,56,128]{2,1,0:T(8,128)(2,1)S(1)}, u32[]{:S(2)}, u32[]{:S(2)}) async-start(bf16[128,56,128]{2,1,0:T(8,128)(2,1)} %pick_pivots.1), calls=%async_computation | async-start | bytes 3670016 | tf_op jit(solution)/shard_map/all_to_all | solution.py:21
  43.7 1.3 copy-start
  48.6 5.9 %copy-start.2 = (s32[32,16,8]{0,2,1:T(8,128)S(1)}, s32[32,16,8]{0,2,1:T(8,128)}, u32[]{:S(2)}) copy-start(s32[32,16,8]{0,2,1:T(8,128)} %param.13) | copy-start | bytes 49156
  48.6 7.5 %copy-start.3 = (s32[32,16,8]{0,2,1:T(8,128)S(1)}, s32[32,16,8]{0,2,1:T(8,128)}, u32[]{:S(2)}) copy-start(s32[32,16,8]{0,2,1:T(8,128)} %param.12) | copy-start | bytes 49156
  48.6 7.5 %copy-start.5 = (s32[32,16]{0,1:T(8,128)S(1)}, s32[32,16]{0,1:T(8,128)}, u32[]{:S(2)}) copy-start(s32[32,16]{0,1:T(8,128)} %param.14) | copy-start | bytes 6148
  48.6 46.7 %all-to-all-start.1 = ((bf16[128,48,256]{2,1,0:T(8,128)(2,1)}), bf16[128,48,256]{2,1,0:T(8,128)(2,1)}, u32[]{:S(2)}, u32[]{:S(2)}) async-start(bf16[128,48,256]{2,1,0:T(8,128)(2,1)} %chosen_rows.1), calls=%async_computation.1 | async-start | bytes 6291456 | tf_op jit(solution)/shard_map/all_to_all | solution.py:21
  54.5 2.0 %copy-start.1 = (f32[512,512]{1,0:T(8,128)S(1)}, f32[512,512]{1,0:T(8,128)}, u32[]{:S(2)}) copy-start(f32[512,512]{1,0:T(8,128)} %param.18) | copy-start | bytes 3145732
  57.1 1.6 copy-start.4

commit v3 on v2

--- a/solution.py
+++ b/solution.py
@@ -218,14 +218,24 @@
         send.wait()
 
 
-def assemble_kernel(rows, radial, got, out, strip, sems):
+def assemble_kernel(rows, radial, got, lower, out, strip, results, sems, sent):
     group, nrow, nmom, nrad = rows.shape
     nstrip = strip.shape[0]
+    npiv = lower.shape[0]
+    wide = results.shape[2]
     copies = strip_copies(got, strip, sems)
     for copy in copies:
         copy.start()
+    low1 = lower[...].astype(BF16)
+    low2 = (lower[...] - low1.astype(F32)).astype(BF16)
+    for i, low in enumerate((low1, low2)):
+        for at in range(0, npiv, wide):
+            results[nrow + i, at // wide * npiv : (at // wide + 1) * npiv, :] = low[:, at : at + wide]
     for copy in copies:
         copy.wait()
+
+    def send(p):
+        return pltpu.make_async_copy(results.at[p], out.at[p], sent.at[p])
 
     def one(p, carry):
         forms = [rows[q, p].astype(F32) for q in range(group)]
@@ -234,63 +244,59 @@
                 [(forms[q] * radial[q, p, j : j + 1, :]).astype(BF16) for q in range(group)], axis=0
             )
             block = lax.dot_general(strip[j], scaled, NT, preferred_element_type=F32)
-            out[p, j * nmom : (j + 1) * nmom, :] = block.astype(BF16)
+            results[p, j * nmom : (j + 1) * nmom, :] = block.astype(BF16)
+        send(p).start()
         return carry
 
+    send(nrow).start()
+    send(nrow + 1).start()
     lax.fori_loop(0, nrow, one, 0)
-
-
-def update_kernel(
-    own, got, lower, blocks, out, upper_t, waves, low, columns, before, upper_all, spread, chosen, results, sems, sent
-):
+    for p in range(nrow + 2):
+        send(p).wait()
+
+
+def update_kernel(own, got, blocks, out, upper_t, low1, low2, before, upper_all, spread, chosen, sems, low_sems):
     npiv, scols = chosen.shape
-    ndev, rows, wide = waves.shape
-    nrow, ncol, deep, _ = columns.shape
-    wave = pltpu.make_async_copy(got.at[:, pl.ds(deep, rows), :], waves, sems.at[2 * nrow])
-    wave.start()
-    bottom = pltpu.make_async_copy(lower, low, sems.at[2 * nrow + 1])
-    bottom.start()
-    loads = []
-    for p in range(nrow):
-        load = (
-            pltpu.make_async_copy(got.at[pl.ds(p * ncol, ncol), pl.ds(0, deep), :], columns.at[p], sems.at[p]),
-            pltpu.make_async_copy(blocks.at[p], before.at[p], sems.at[nrow + p]),
-        )
-        for copy in load:
-            copy.start()
-        loads.append(load)
-    wave.wait()
+    ndev, deep2, wide = got.shape
+    nrow = before.shape[0]
+    ncol = ndev // nrow
+    deep = npiv // ncol
+    rows = deep2 - deep
+    lows = []
+    for i, low in enumerate((low1, low2)):
+        for h in range(npiv // wide):
+            lows.append(
+                pltpu.make_async_copy(
+                    blocks.at[nrow + i, pl.ds(h * npiv, npiv), :], low.at[:, pl.ds(h * wide, wide)], low_sems.at[i, h]
+                )
+            )
+    loads = [pltpu.make_async_copy(blocks.at[p], before.at[p], sems.at[p]) for p in range(nrow)]
+    for load in lows + loads:
+        load.start()
     for b in range(wide // LANES):
-        spread[b] = waves[:, :, b * LANES : (b + 1) * LANES].astype(F32).reshape(ndev * rows, LANES)
+        spread[b] = got[:, deep:, b * LANES : (b + 1) * LANES].astype(F32).reshape(ndev * rows, LANES)
         for h in range(scols // wide):
             start = h * wide + b * LANES
             for a in range(own):
                 chosen[a * ndev : (a + 1) * ndev, start : start + LANES] = spread[
                     b, pl.ds(h * own + a, ndev, stride=rows), :
                 ].astype(BF16)
-    bottom.wait()
-    low1 = low[...].astype(BF16)
-    low2 = (low[...] - low1.astype(F32)).astype(BF16)
+    for load in lows:
+        load.wait()
     for at in range(0, scols, wide):
         rows_of = chosen[:, at : at + wide]
-        upper = jnp.dot(low1, rows_of, preferred_element_type=F32) + jnp.dot(
-            low2, rows_of, preferred_element_type=F32
+        upper = jnp.dot(low1[...], rows_of, preferred_element_type=F32) + jnp.dot(
+            low2[...], rows_of, preferred_element_type=F32
         )
         upper_all[at : at + wide, :] = upper.T.astype(BF16)
     width = upper_t.shape[0]
     upper_t[...] = upper_all[pl.ds(pl.multiple_of(lax.axis_index("col") * width, width), width), :]
     for load in loads:
-        for copy in load:
-            copy.wait()
-    sends = []
+        load.wait()
     for p in range(nrow):
-        change = jnp.dot(upper_all[...], columns[p].reshape(npiv, wide), preferred_element_type=F32)
-        results[p] = (before[p].astype(F32) - change).astype(BF16)
-        send = pltpu.make_async_copy(results.at[p], out.at[p], sent.at[p])
-        send.start()
-        sends.append(send)
-    for send in sends:
-        send.wait()
+        columns = got[p * ncol : (p + 1) * ncol, :deep, :].reshape(npiv, wide)
+        change = jnp.dot(upper_all[...], columns, preferred_element_type=F32)
+        out[p] = (before[p].astype(F32) - change).astype(BF16)
 
 
 def widen_kernel(got, out, broad, sent):
@@ -394,7 +400,7 @@
             dma((ndev // many,)),
         ],
         input_output_aliases={3: 0},
-        compiler_params=room(61),
+        compiler_params=room(40),
         cost_estimate=cost(2 * own * nstrip * scols * nrad, 4 << 20),
         name="chosen_rows",
     )(got, kernels, angular_coef[:, None], second)
@@ -404,42 +410,46 @@
     lam = jnp.where(position < term_count[:, :, None], lam_index, nlam)
     mixing = mixing_weights(lam, coef_index, angular_coef, nlam)
     radial = weights_to_radial(mixing, kernels)
+    lower = lower_inverse.reshape(npiv, ndev, own).transpose(0, 2, 1).reshape(npiv, npiv)
+    slots = 10 * nrow
     blocks = pl.pallas_call(
         assemble_kernel,
-        out_shape=jax.ShapeDtypeStruct((nrow, scols, group * nmom), BF16),
-        in_specs=[vmem, vmem, anywhere],
-        out_specs=vmem,
-        scratch_shapes=[pltpu.VMEM((nstrip, nmom, nrad), BF16), dma((nrow,))],
+        out_shape=jax.ShapeDtypeStruct((slots, scols, group * nmom), BF16),
+        in_specs=[vmem, vmem, anywhere, vmem],
+        out_specs=anywhere,
+        scratch_shapes=[
+            pltpu.VMEM((nstrip, nmom, nrad), BF16),
+            pltpu.VMEM((nrow + 2, scols, group * nmom), BF16),
+            dma((nrow,)),
+            dma((nrow + 2,)),
+        ],
         compiler_params=room(56),
         cost_estimate=cost(2 * local * scols * nrad * 4, 8 << 20),
         name="assemble_strip",
-    )(form_rows.reshape(group, nrow, nmom, nrad), radial.reshape(group, nrow, nstrip, nrad), got)
-
-    lower = lower_inverse.reshape(npiv, ndev, own).transpose(0, 2, 1).reshape(npiv, npiv)
+    )(form_rows.reshape(group, nrow, nmom, nrad), radial.reshape(group, nrow, nstrip, nrad), got, lower)
+
     done, upper_t = pl.pallas_call(
         functools.partial(update_kernel, own),
         out_shape=(
             jax.ShapeDtypeStruct((nrow, scols, wide), BF16),
             jax.ShapeDtypeStruct((width, npiv), BF16),
         ),
-        in_specs=[anywhere, anywhere, anywhere],
-        out_specs=(anywhere, vmem),
+        in_specs=[vmem, anywhere],
+        out_specs=(vmem, vmem),
         scratch_shapes=[
-            pltpu.VMEM((ndev, wave_rows, wide), BF16),
-            pltpu.VMEM((npiv, npiv), F32),
-            pltpu.VMEM((nrow, ncol, deep, wide), BF16),
+            pltpu.VMEM((npiv, npiv), BF16),
+            pltpu.VMEM((npiv, npiv), BF16),
             pltpu.VMEM((nrow, scols, wide), BF16),
             pltpu.VMEM((scols, npiv), BF16),
             pltpu.VMEM((wide // LANES, ndev * wave_rows, LANES), F32),
             pltpu.VMEM((npiv, scols), BF16),
-            pltpu.VMEM((nrow, scols, wide), BF16),
-            dma((2 * nrow + 2,)),
             dma((nrow,)),
+            dma((2, npiv // wide)),
         ],
-        compiler_params=room(56),
+        compiler_params=room(24),
         cost_estimate=cost(2 * npiv * scols * (3 * npiv + local), 12 << 20),
         name="update_blocks",
-    )(got2, lower, blocks)
+    )(got2, blocks)
     final = exchange(done.reshape(ndev, width, wide))
     steps = 16
     trailing = pl.pallas_call(

time: 164 us -> 160 us (0.976)
  waiting for transfers between devices: 40.8 us -> 30.6 us
  local copies, waits for them, and re-layouts: 8.54 us -> 16.2 us
  Pallas kernels: 35.6 us -> 32.3 us
  other arithmetic: 1.49 us -> 3.89 us
    all_to_all x2, waiting for transfers between devices: 40.8 us -> 30.6 us  [exchange(): return lax.all_to_all(chunks, ALL, split_axis=0, concat_axis=0, tiled=True)]
    unnamed x17 -> x15, local copies, waits for them, and re-layouts: 2.87 us -> 5.72 us
    reshape x1, local copies, waits for them, and re-layouts: 0.31 us -> 2.5 us  [shards(): lower_inverse.reshape(npiv, ndev, own).transpose(0, 2, 1)]
    transpose x1, local copies, waits for them, and re-layouts: 0.58 us -> 2.27 us  [shards(): lower_inverse.reshape(npiv, ndev, own).transpose(0, 2, 1)]
  transfers between devices with their start and end apart: 2 -> 2, of which waited for: 2 -> 2; matrix products, arithmetic and copies ran while one was open for 6% -> 14% of each run, Pallas kernels for 10% -> 10%
where the time goes in v3:
time: 160 us; the launch traced here: 159 us
  blocking collectives  57 us (36%)
  Pallas kernels  32.3 us (20%)
  waiting for transfers between devices  30.6 us (19%)
  starting transfers between devices  16.3 us (10%)
  local copies, waits for them, and re-layouts  16.2 us (10%)
  other arithmetic  3.89 us (2%)
  matrix products  1.97 us (1%)
    all_to_all x1, blocking collectives, exchange(): return lax.all_to_all(chunks, ALL, split_axis=0, concat_axis=0, tiled=True)  57 us
    all_to_all x2, waiting for transfers between devices, exchange(): return lax.all_to_all(chunks, ALL, split_axis=0, concat_axis=0, tiled=True)  30.6 us
    all_to_all x2, starting transfers between devices, exchange(): return lax.all_to_all(chunks, ALL, split_axis=0, concat_axis=0, tiled=True)  16.3 us
    pallas_call x1, Pallas kernels, shards(): pl.pallas_call(assemble_kernel, out_shape=jax.ShapeDtypeStruct((slots, sc...  15.5 us
    pallas_call x1, Pallas kernels, shards(): pl.pallas_call(functools.partial(update_kernel, own), out_shape=(jax.Shap...  6.12 us
    unnamed x15, local copies, waits for them, and re-layouts  5.72 us
    pallas_call x1, Pallas kernels, shards(): pl.pallas_call(functools.partial(pick_kernel, own), out_shape=jax.ShapeDt...  4.6 us
    pallas_call x1, Pallas kernels, shards(): pl.pallas_call(widen_kernel, out_shape=jax.ShapeDtypeStruct((width, ndev...  3.45 us
  transfers between devices with their start and end apart: 2, of which 2 were waited for; matrix products, arithmetic and copies ran while one was open for 14% of the time, Pallas kernels for 10%

profile of v3, /device:TPU:1, one launch (start us, length us, event | category | flops | bytes accessed | tf_op | source)
XLA Modules:
  0.0 159.1 jit_solution(17111886368013181084)
XLA Ops:
  0.6 4.6 %pick_pivots.1 = bf16[128,56,128]{2,1,0:T(8,128)(2,1)} custom-call(s32[1,512]{1,0:T(1,128)} %bitcast.45, s32[128,32]{1,0:T(8,128)} %bitcast.43, s32[128,32]{1,0:T(8,128)} %bitcast.42, s32[16,32]{1,0:T(8,128)} %bitcast.44, bf16[2048,512]{1,0:T(8,128)(2,1)} %bitcast.34, bf16[1,64,512]{2,1,0:T(8,128)(2,1)} %form_strip_at.1), custom_call_target="tpu_custom_call" | custom-call | flops 1073741824 | bytes 4194304 | tf_op jit(solution)/shard_map/pick_pivots/pallas_call | solution.py:352
  5.2 0.0 copy-start.5
  5.3 11.5 %all-to-all-start = ((bf16[128,56,128]{2,1,0:T(8,128)(2,1)}), bf16[128,56,128]{2,1,0:T(8,128)(2,1)S(1)}, u32[]{:S(2)}, u32[]{:S(2)}) async-start(bf16[128,56,128]{2,1,0:T(8,128)(2,1)} %pick_pivots.1), calls=%async_computation | async-start | bytes 3670016 | tf_op jit(solution)/shard_map/all_to_all | solution.py:21
  16.8 0.0 copy-done.5
  16.8 0.1 copy.31.angular_at
  16.9 1.9 %copy.42 = bf16[4,128,8,256]{3,2,0,1:T(8,128)(2,1)S(1)} copy(bf16[4,128,8,256]{3,2,1,0:T(8,128)(2,1)} %bitcast.40) | data formatting | bytes 4194304 | tf_op jit(solution)/shard_map/reshape | solution.py:384
  18.7 0.0 copy-start.1
  18.8 1.9 %pad.4.kept = bf16[128,48,256]{2,1,0:T(8,128)(2,1)} pad(bf16[128,32,256]{2,1,0:T(8,128)(2,1)S(1)} %bitcast.36, bf16[]{:T(256)} %constant.6.clone.1), padding=0_0x0_16x0_0 | pad | bytes 5242882 | tf_op jit(solution)/shard_map/jit(_pad)/pad | solution.py:386
  20.6 23.1 %all-to-all-done.got = bf16[128,56,128]{2,1,0:T(8,128)(2,1)S(1)} async-done(((bf16[128,56,128]{2,1,0:T(8,128)(2,1)}), bf16[128,56,128]{2,1,0:T(8,128)(2,1)S(1)}, u32[]{:S(2)}, u32[]{:S(2)}) %all-to-all-start) | async-done | bytes 1835040 | tf_op jit(solution)/shard_map/all_to_all | solution.py:21
  43.7 0.0 copy-done.1
  43.7 0.0 copy-start
  43.7 2.7 %chosen_rows.1 = bf16[128,48,256]{2,1,0:T(8,128)(2,1)} custom-call(bf16[128,56,128]{2,1,0:T(8,128)(2,1)S(1)} %all-to-all-done.got, f32[16,512]{1,0:T(8,128)S(1)} %copy-done.1, f32[64,1]{1,0:T(8,128)S(1)} %copy.31.angular_at, bf16[128,48,256]{2,1,0:T(8,128)(2,1)} %pad.4.kept), custom_call_target="tpu_custom_call", output_to_operand_aliasing={{}: (3, {})} | custom-call | flops 67108864 | bytes 4194304 | tf_op jit(solution)/shard_map/chosen_rows/pallas_call | solution.py:388
  46.4 0.0 copy-done
  46.4 0.0 copy-start.2
  46.4 0.0 copy-start.3
  46.5 0.0 copy-start.4
  46.5 4.8 %all-to-all-start.1 = ((bf16[128,48,256]{2,1,0:T(8,128)(2,1)}), bf16[128,48,256]{2,1,0:T(8,128)(2,1)S(1)}, u32[]{:S(2)}, u32[]{:S(2)}) async-start(bf16[128,48,256]{2,1,0:T(8,128)(2,1)} %chosen_rows.1), calls=%async_computation.1 | async-start | bytes 6291456 | tf_op jit(solution)/shard_map/all_to_all | solution.py:21
  51.3 0.0 copy-done.2
  51.3 0.8 copy.32
  52.1 2.2 %select_reduce_fusion = f32[32,16,8]{2,1,0:T(8,128)S(1)} fusion(f32[64]{0:T(128)S(1)} %copy-done.5, s32[32,16,8]{2,1,0:T(8,128)} %copy.32), kind=kLoop, calls=%fused_computation.1 | loop fusion | flops 782336 | bytes 33024 | tf_op jit(solution)/shard_map/reduce_sum | solution.py:30
  54.4 0.8 copy.33
  55.2 0.0 copy-done.3
  55.2 0.0 copy-done.4
  55.2 1.6 %select_reduce_fusion.1 = f32[32,16,16]{0,2,1:T(8,128)} fusion(f32[32,16,8]{0,2,1:T(8,128)} %copy.33, s32[32,16,8]{0,2,1:T(8,128)S(1)} %fusion), kind=kLoop, calls=%fused_computation.4 | loop fusion | flops 188416 | bytes 65536 | tf_op jit(solution)/shard_map/reduce_sum | solution.py:32
  56.8 1.1 copy.34
  57.9 2.6 %copy.35 = f32[512,512]{0,1:T(8,128)} copy(f32[512,512]{1,0:T(8,128)} %param.18) | data formatting | bytes 2097152 | tf_op args[8]
  60.5 2.5 %reshape.41 = f32[512,128,4]{0,2,1:T(4,128)} reshape(f32[512,512]{0,1:T(8,128)} %copy.35) | data formatting | bytes 2097152 | tf_op jit(solution)/shard_map/reshape | solution.py:413
  63.0 2.3 %copy.36 = f32[512,4,128]{2,1,0:T(4,128)} copy(f32[512,4,128]{0,1,2:T(4,128)} %bitcast.38) | data formatting | bytes 2097152 | tf_op jit(solution)/shard_map/transpose | solution.py:413
  65.3 2.3 %copy.43 = f32[64,8,4,128]{3,1,2,0:T(8,128)} copy(f32[64,8,4,128]{3,2,1,0:T(4,128)} %bitcast.39) | data formatting | bytes 2097152
  67.5 2.0 %fusion.1.radial = f32[4,8,16,512]{3,2,1,0:T(8,128)} fusion(f32[4,8,16,16]{3,2,1,0:T(8,128)S(1)} %bitcast.41, f32[16,512]{1,0:T(8,128)S(1)} %copy-done.1), kind=kOutput, calls=%fused_computation.8 | convolution fusion | flops 50331648 | bytes 1114112 | tf_op jit(solution)/shard_map/dot_general | solution.py:37
  69.5 15.5 %assemble_strip.1.blocks = bf16[80,1024,256]{2,1,0:T(8,128)(2,1)} custom-call(bf16[4,8,64,512]{3,2,1,0:T(8,128)(2,1)} %bitcast.35, f32[4,8,16,512]{3,2,1,0:T(8,128)} %fusion.1.radial, bf16[128,56,128]{2,1,0:T(8,128)(2,1)} %copy-done, f32[512,512]{1,0:T(8,128)} %bitcast.37), custom_call_target="tpu_custom_call" | custom-call | flops 8589934592 | bytes 8388608 | tf_op jit(solution)/shard_map/assemble_strip/pallas_call | solution.py:415
  85.0 7.5 %all-to-all-done.1.got = bf16[128,48,256]{2,1,0:T(8,128)(2,1)S(1)} async-done(((bf16[128,48,256]{2,1,0:T(8,128)(2,1)}), bf16[128,48,256]{2,1,0:T(8,128)(2,1)S(1)}, u32[]{:S(2)}, u32[]{:S(2)}) %all-to-all-start.1) | async-done | bytes 3145760 | tf_op jit(solution)/shard_map/all_to_all | solution.py:21
  92.5 6.1 %update_blocks.1 = (bf16[8,1024,256]{2,1,0:T(8,128)(2,1)S(1)}, bf16[64,512]{1,0:T(8,128)(2,1)}) custom-call(bf16[128,48,256]{2,1,0:T(8,128)(2,1)S(1)} %all-to-all-done.1.got, bf16[80,1024,256]{2,1,0:T(8,128)(2,1)} %assemble_strip.1.blocks), custom_call_target="tpu_custom_call" | custom-call | flops 3758096384 | bytes 12582912 | tf_op jit(solution)/shard_map/update_blocks/pallas_call | solution.py:431
  98.6 57.0 %all_to_all.15.got = bf16[128,64,256]{2,1,0:T(8,128)(2,1)S(1)} all-to-all(bf16[128,64,256]{2,1,0:T(8,128)(2,1)S(1)} %bitcast.33), channel_id=1, replica_groups=mesh['row'=8,'col'=16] {'row','col'}, dimensions={0} | all-to-all | bytes 8388608 | tf_op jit(solution)/shard_map/all_to_all | solution.py:21
  155.5 3.4 %widen_blocks.1 = f32[64,32768]{1,0:T(8,128)} custom-call(bf16[128,64,256]{2,1,0:T(8,128)(2,1)S(1)} %all_to_all.15.got), custom_call_target="tpu_custom_call" | custom-call | flops 2097152 | bytes 12582912 | tf_op jit(solution)/shard_map/widen_blocks/pallas_call | solution.py:455
  (1 shorter events, 0.0 us)
Async XLA Ops:
  5.2 11.5 %copy-start.5 = (f32[64]{0:T(128)S(1)}, f32[64]{0:T(128)}, u32[]{:S(2)}) copy-start(f32[64]{0:T(128)} %param.15) | copy-start | bytes 772
  5.3 38.5 %all-to-all-start = ((bf16[128,56,128]{2,1,0:T(8,128)(2,1)}), bf16[128,56,128]{2,1,0:T(8,128)(2,1)S(1)}, u32[]{:S(2)}, u32[]{:S(2)}) async-start(bf16[128,56,128]{2,1,0:T(8,128)(2,1)} %pick_pivots.1), calls=%async_computation | async-start | bytes 3670016 | tf_op jit(solution)/shard_map/all_to_all | solution.py:21
  18.7 25.0 %copy-start.1 = (f32[16,512]{1,0:T(8,128)S(1)}, f32[16,512]{1,0:T(8,128)}, u32[]{:S(2)}) copy-start(f32[16,512]{1,0:T(8,128)} %kernels_at.1) | copy-start | bytes 98308
  43.7 2.7 %copy-start = (bf16[128,56,128]{2,1,0:T(8,128)(2,1)}, bf16[128,56,128]{2,1,0:T(8,128)(2,1)S(1)}, u32[]{:S(2)}) copy-start(bf16[128,56,128]{2,1,0:T(8,128)(2,1)S(1)} %all-to-all-done.got) | copy-start | bytes 5505028
  46.4 4.9 %copy-start.2 = (s32[32,16,8]{0,2,1:T(8,128)S(1)}, s32[32,16,8]{0,2,1:T(8,128)}, u32[]{:S(2)}) copy-start(s32[32,16,8]{0,2,1:T(8,128)} %param.13) | copy-start | bytes 49156
  46.4 8.7 %copy-start.3 = (s32[32,16,8]{0,2,1:T(8,128)S(1)}, s32[32,16,8]{0,2,1:T(8,128)}, u32[]{:S(2)}) copy-start(s32[32,16,8]{0,2,1:T(8,128)} %param.12) | copy-start | bytes 49156
  46.5 8.7 %copy-start.4 = (s32[32,16]{0,1:T(8,128)S(1)}, s32[32,16]{0,1:T(8,128)}, u32[]{:S(2)}) copy-start(s32[32,16]{0,1:T(8,128)} %param.14) | copy-start | bytes 6148
  46.5 46.0 %all-to-all-start.1 = ((bf16[128,48,256]{2,1,0:T(8,128)(2,1)}), bf16[128,48,256]{2,1,0:T(8,128)(2,1)S(1)}, u32[]{:S(2)}, u32[]{:S(2)}) async-start(bf16[128,48,256]{2,1,0:T(8,128)(2,1)} %chosen_rows.1), calls=%async_computation.1 | async-start | bytes 6291456 | tf_op jit(solution)/shard_map/all_to_all | solution.py:21

commit v4 on v3

--- a/solution.py
+++ b/solution.py
@@ -9,6 +9,7 @@
 
 ALL = ("row", "col")
 LANES = 128
+CORES = 2
 BF16, F32 = jnp.bfloat16, jnp.float32
 NT = (((1,), (1,)), ((), ()))
 
@@ -81,14 +82,17 @@
     for load in loads:
         load.wait()
     tall = deep1 - own * acc.shape[1] // LANES
-    halves = nmom // tall
-    half, part = lax.rem(row, halves), lax.div(row, halves)
-    share = form_strip[
-        0,
-        pl.ds(pl.multiple_of(half * tall, tall), tall),
-        pl.ds(pl.multiple_of(part * LANES, LANES), LANES),
-    ]
-    chunks[:, :tall, :] = jnp.broadcast_to(share[None], (ndev, tall, LANES))
+    ncol = lax.axis_size("col")
+    half, part = lax.rem(row, CORES), lax.div(row, CORES)
+    for core in range(CORES):
+        start = half * CORES * tall + core * tall
+        share = form_strip[
+            0,
+            pl.ds(pl.multiple_of(start, tall), tall),
+            pl.ds(pl.multiple_of(part * LANES, LANES), LANES),
+        ]
+        for at in range(core * ncol, ndev, CORES * ncol):
+            chunks[at : at + ncol, :tall, :] = jnp.broadcast_to(share[None], (ncol, tall, LANES))
     column = jnp.broadcast_to(pivots[...].astype(F32), (LANES, npiv)).T[:, :1].astype(jnp.int32) - me * local
     counts = jnp.broadcast_to(count[...][:, None, :], (nstrip, terms, chans)).reshape(nstrip * terms, chans)
     position = lax.rem(lax.broadcasted_iota(jnp.int32, (nstrip * terms, chans), 0), terms)
@@ -126,38 +130,36 @@
         send.wait()
 
 
-def strip_copies(got, strip, sems):
+def strip_copies(got, other, strip, sems):
     nstrip, nmom, nrad = strip.shape
     nrow = got.shape[0] // nstrip
-    halves = nrow * LANES // nrad
-    tall = nmom // halves
-    return [
-        pltpu.make_async_copy(
-            got.at[pl.ds(row * nstrip, nstrip), pl.ds(0, tall), :],
-            strip.at[:, pl.ds(row % halves * tall, tall), pl.ds(row // halves * LANES, LANES)],
-            sems.at[row],
-        )
-        for row in range(nrow)
+    tall = nmom // (CORES * CORES)
+    core = lax.rem(lax.axis_index("row"), CORES)
+    copies = []
+    for i, (source, side) in enumerate(((got, core), (other, 1 - core))):
+        for row in range(nrow):
+            start = pl.multiple_of(row % CORES * CORES * tall + side * tall, tall)
+            copies.append(
+                pltpu.make_async_copy(
+                    source.at[pl.ds(row * nstrip, nstrip), pl.ds(0, tall), :],
+                    strip.at[:, pl.ds(start, tall), pl.ds(row // CORES * LANES, LANES)],
+                    sems.at[i * nrow + row],
+                )
+            )
+    return copies
+
+
+def scale_kernel(own, nstrip, got, kernels_at, angular_at, scaled, mail, kernels, angular, loads):
+    ndev, deep1, _ = got.shape
+    nrad = kernels.shape[1]
+    parts = nrad // LANES
+    rows = mail.shape[1]
+    first = [
+        pltpu.make_async_copy(got.at[:, pl.ds(deep1 - rows, rows), :], mail, loads.at[0]),
+        pltpu.make_async_copy(kernels_at, kernels, loads.at[1]),
+        pltpu.make_async_copy(angular_at, angular, loads.at[2]),
     ]
-
-
-def chosen_kernel(
-    own, got, kernels_at, angular_at, kept, second, mail, kernels, angular, strip, wave, loads, sent
-):
-    del kept
-    nstrip, nmom, nrad = strip.shape
-    ndev, deep1, _ = got.shape
-    nrow = ndev // nstrip
-    parts = nrad // LANES
-    halves = nrow // parts
-    tall = nmom // halves
-    first = [
-        pltpu.make_async_copy(got.at[:, pl.ds(tall, deep1 - tall), :], mail, loads.at[nrow]),
-        pltpu.make_async_copy(kernels_at, kernels, loads.at[nrow + 1]),
-        pltpu.make_async_copy(angular_at, angular, loads.at[nrow + 2]),
-    ]
-    later = strip_copies(got, strip, loads)
-    for copy in first + later:
+    for copy in first:
         copy.start()
     for copy in first:
         copy.wait()
@@ -191,11 +193,20 @@
         preferred_element_type=F32,
     )
     radial = jnp.dot(mixing, kernels[...], precision=lax.Precision.HIGHEST, preferred_element_type=F32)
-    scaled = (jnp.concatenate(forms, axis=0) * radial).astype(BF16)
+    scaled[...] = (jnp.concatenate(forms, axis=0) * radial).astype(BF16)
+
+
+def chosen_kernel(own, got, other, scaled, kept, second, strip, wave, loads, sent):
+    del kept
+    nstrip, nmom, nrad = strip.shape
+    ndev = got.shape[0]
+    copies = strip_copies(got, other, strip, loads)
+    for copy in copies:
+        copy.start()
+    for copy in copies:
+        copy.wait()
     scols = nstrip * nmom
-    for copy in later:
-        copy.wait()
-    full = lax.dot_general(scaled, strip[...].reshape(scols, nrad), NT, preferred_element_type=F32)
+    full = lax.dot_general(scaled[...], strip[...].reshape(scols, nrad), NT, preferred_element_type=F32)
     keep = (
         lax.broadcasted_iota(jnp.int32, (nstrip, scols), 0)
         == lax.broadcasted_iota(jnp.int32, (nstrip, scols), 1) // nmom
@@ -218,12 +229,12 @@
         send.wait()
 
 
-def assemble_kernel(rows, radial, got, lower, out, strip, results, sems, sent):
+def assemble_kernel(rows, radial, got, other, lower, out, strip, results, sems, sent):
     group, nrow, nmom, nrad = rows.shape
     nstrip = strip.shape[0]
     npiv = lower.shape[0]
     wide = results.shape[2]
-    copies = strip_copies(got, strip, sems)
+    copies = strip_copies(got, other, strip, sems)
     for copy in copies:
         copy.start()
     low1 = lower[...].astype(BF16)
@@ -343,9 +354,7 @@
     anywhere = pl.BlockSpec(memory_space=pl.ANY)
     dma = pltpu.SemaphoreType.DMA
 
-    parts = nrad // LANES
-    halves = nrow // parts
-    tall = nmom // halves
+    tall = nmom // (CORES * CORES)
     extra = 2 * nstrip * terms
     deep1 = tall + own * (nrad + extra) // LANES
     steps, groups = 4, 4
@@ -378,32 +387,46 @@
         form_rows.reshape(local, nrad),
         form_strip,
     )
-    got = exchange(first)
-
     deep, wide = panel.shape[0], panel.shape[1] // ndev
     cut = panel.reshape(deep, ndev, wide).transpose(1, 0, 2)
     wave_rows = own * scols // wide
     second = jnp.pad(cut, ((0, 0), (0, wave_rows), (0, 0)))
+    got = exchange(first)
+    got, second = lax.optimization_barrier((got, second))
+    other = lax.ppermute(got, "row", [(i, i ^ 1) for i in range(nrow)])
+
     many = 32
-    second = pl.pallas_call(
-        functools.partial(chosen_kernel, own),
-        out_shape=jax.ShapeDtypeStruct(second.shape, BF16),
-        in_specs=[anywhere] * 4,
-        out_specs=anywhere,
+    scaled = pl.pallas_call(
+        functools.partial(scale_kernel, own, nstrip),
+        out_shape=jax.ShapeDtypeStruct((own * nstrip, nrad), BF16),
+        in_specs=[anywhere] * 3,
+        out_specs=vmem,
         scratch_shapes=[
             pltpu.VMEM((ndev, deep1 - tall, LANES), BF16),
             pltpu.VMEM(kernels.shape, F32),
             pltpu.VMEM((angular_coef.shape[0], 1), F32),
+            dma((3,)),
+        ],
+        compiler_params=room(40),
+        cost_estimate=cost(2 * own * nstrip * nrad * LANES, 1 << 20),
+        name="scale_pivots",
+    )(got, kernels, angular_coef[:, None])
+    second = pl.pallas_call(
+        functools.partial(chosen_kernel, own),
+        out_shape=jax.ShapeDtypeStruct(second.shape, BF16),
+        in_specs=[anywhere, anywhere, vmem, anywhere],
+        out_specs=anywhere,
+        scratch_shapes=[
             pltpu.VMEM((nstrip, nmom, nrad), BF16),
             pltpu.VMEM((many, wave_rows, wide), BF16),
-            dma((nrow + 3,)),
+            dma((CORES * nrow,)),
             dma((ndev // many,)),
         ],
         input_output_aliases={3: 0},
         compiler_params=room(40),
         cost_estimate=cost(2 * own * nstrip * scols * nrad, 4 << 20),
         name="chosen_rows",
-    )(got, kernels, angular_coef[:, None], second)
+    )(got, other, scaled, second)
     got2 = exchange(second)
 
     position = lax.broadcasted_iota(jnp.int32, lam_index.shape, 2)
@@ -415,18 +438,18 @@
     blocks = pl.pallas_call(
         assemble_kernel,
         out_shape=jax.ShapeDtypeStruct((slots, scols, group * nmom), BF16),
-        in_specs=[vmem, vmem, anywhere, vmem],
+        in_specs=[vmem, vmem, anywhere, anywhere, vmem],
         out_specs=anywhere,
         scratch_shapes=[
             pltpu.VMEM((nstrip, nmom, nrad), BF16),
             pltpu.VMEM((nrow + 2, scols, group * nmom), BF16),
-            dma((nrow,)),
+            dma((CORES * nrow,)),
             dma((nrow + 2,)),
         ],
         compiler_params=room(56),
         cost_estimate=cost(2 * local * scols * nrad * 4, 8 << 20),
         name="assemble_strip",
-    )(form_rows.reshape(group, nrow, nmom, nrad), radial.reshape(group, nrow, nstrip, nrad), got, lower)
+    )(form_rows.reshape(group, nrow, nmom, nrad), radial.reshape(group, nrow, nstrip, nrad), got, other, lower)
 
     done, upper_t = pl.pallas_call(
         functools.partial(update_kernel, own),

time: 160 us -> 156 us (0.975)
  local copies, waits for them, and re-layouts: 16.2 us -> 14 us
  waiting for transfers between devices: 30.6 us -> 28.8 us
    all_to_all x2, waiting for transfers between devices: 30.6 us -> 27.3 us  [exchange(): return lax.all_to_all(chunks, ALL, split_axis=0, concat_axis=0, tiled=True)]
    unnamed x15 -> x17, local copies, waits for them, and re-layouts: 5.72 us -> 5.72 us
  transfers between devices with their start and end apart: 2 -> 3, of which waited for: 2 -> 3; matrix products, arithmetic and copies ran while one was open for 14% -> 13% of each run, Pallas kernels for 10% -> 11%
where the time goes in v4:
time: 156 us
  blocking collectives  57 us (37%)
  Pallas kernels  32.2 us (21%)
  waiting for transfers between devices  28.8 us (18%)
  starting transfers between devices  17 us (11%)
  local copies, waits for them, and re-layouts  14 us (9%)
  other arithmetic  3.88 us (2%)
  matrix products  1.95 us (1%)
    all_to_all x1, blocking collectives, exchange(): return lax.all_to_all(chunks, ALL, split_axis=0, concat_axis=0, tiled=True)  57 us
    all_to_all x2, waiting for transfers between devices, exchange(): return lax.all_to_all(chunks, ALL, split_axis=0, concat_axis=0, tiled=True)  27.3 us
    all_to_all x2, starting transfers between devices, exchange(): return lax.all_to_all(chunks, ALL, split_axis=0, concat_axis=0, tiled=True)  15.5 us
    pallas_call x1, Pallas kernels, shards(): pl.pallas_call(assemble_kernel, out_shape=jax.ShapeDtypeStruct((slots, sc...  15.5 us
    pallas_call x1, Pallas kernels, shards(): pl.pallas_call(functools.partial(update_kernel, own), out_shape=(jax.Shap...  6.11 us
    unnamed x17, local copies, waits for them, and re-layouts  5.72 us
    pallas_call x1, Pallas kernels, shards(): pl.pallas_call(functools.partial(pick_kernel, own), out_shape=jax.ShapeDt...  4.36 us
    pallas_call x1, Pallas kernels, shards(): pl.pallas_call(widen_kernel, out_shape=jax.ShapeDtypeStruct((width, ndev...  3.45 us
  transfers between devices with their start and end apart: 3, of which 3 were waited for; matrix products, arithmetic and copies ran while one was open for 13% of the time, Pallas kernels for 11%

profile of v4, /device:TPU:1, one launch (start us, length us, event | category | flops | bytes accessed | tf_op | source)
XLA Modules:
  0.0 155.8 jit_solution(3565250842438916943)
XLA Ops:
  0.6 4.4 %pick_pivots.1 = bf16[128,40,128]{2,1,0:T(8,128)(2,1)} custom-call(s32[1,512]{1,0:T(1,128)} %bitcast.46, s32[128,32]{1,0:T(8,128)} %bitcast.43, s32[128,32]{1,0:T(8,128)} %bitcast.42, s32[16,32]{1,0:T(8,128)} %bitcast.44, bf16[2048,512]{1,0:T(8,128)(2,1)} %bitcast.38, bf16[1,64,512]{2,1,0:T(8,128)(2,1)} %form_strip_at.1), custom_call_target="tpu_custom_call" | custom-call | flops 1073741824 | bytes 4194304 | tf_op jit(solution)/shard_map/pick_pivots/pallas_call | solution.py:361
  5.0 0.0 copy-start.3
  5.0 11.5 %all-to-all-start = ((bf16[128,40,128]{2,1,0:T(8,128)(2,1)}), bf16[128,40,128]{2,1,0:T(8,128)(2,1)S(1)}, u32[]{:S(2)}, u32[]{:S(2)}) async-start(bf16[128,40,128]{2,1,0:T(8,128)(2,1)} %pick_pivots.1), calls=%async_computation | async-start | bytes 2621440 | tf_op jit(solution)/shard_map/all_to_all | solution.py:22
  16.5 0.0 copy-done.3
  16.5 0.3 copy.42
  16.8 0.0 copy-start.6
  16.8 0.0 copy-start.2
  16.8 1.9 %pad.4.kept = bf16[128,48,256]{2,1,0:T(8,128)(2,1)} pad(bf16[128,32,256]{2,1,0:T(8,128)(2,1)S(1)} %bitcast.34, bf16[]{:T(256)} %constant.6.clone.1), padding=0_0x0_16x0_0 | pad | bytes 5242882 | tf_op jit(solution)/shard_map/jit(_pad)/pad | solution.py:393
  18.7 19.1 %all-to-all-done.got = bf16[128,40,128]{2,1,0:T(8,128)(2,1)S(1)} async-done(((bf16[128,40,128]{2,1,0:T(8,128)(2,1)}), bf16[128,40,128]{2,1,0:T(8,128)(2,1)S(1)}, u32[]{:S(2)}, u32[]{:S(2)}) %all-to-all-start) | async-done | bytes 1310752 | tf_op jit(solution)/shard_map/all_to_all | solution.py:22
  37.9 0.0 copy-start
  37.9 1.5 collective-permute-start
  39.4 0.0 copy-done.6
  39.4 0.1 copy.31.angular_at
  39.5 0.0 copy-done.2
  39.5 1.0 scale_pivots.1.scaled
  40.4 1.6 %collective-permute-done.other = bf16[128,40,128]{2,1,0:T(8,128)(2,1)S(1)} collective-permute-done((bf16[128,40,128]{2,1,0:T(8,128)(2,1)S(1)}, bf16[128,40,128]{2,1,0:T(8,128)(2,1)S(1)}, u32[]{:S(2)}, u32[]{:S(2)}) %collective-permute-start) | collective-permute-done | bytes 1310752 | tf_op jit(solution)/shard_map/ppermute | solution.py:396
  42.0 0.0 copy-start.1
  42.0 1.9 %chosen_rows.1 = bf16[128,48,256]{2,1,0:T(8,128)(2,1)} custom-call(bf16[128,40,128]{2,1,0:T(8,128)(2,1)S(1)} %all-to-all-done.got, bf16[128,40,128]{2,1,0:T(8,128)(2,1)S(1)} %collective-permute-done.other, bf16[64,512]{1,0:T(8,128)(2,1)S(1)} %scale_pivots.1.scaled, bf16[128,48,256]{2,1,0:T(8,128)(2,1)} %pad.4.kept), custom_call_target="tpu_custom_call", output_to_operand_aliasing={{}: (3, {})} | custom-call | flops 67108864 | bytes 4194304 | tf_op jit(solution)/shard_map/chosen_rows/pallas_call | solution.py:414
  43.9 0.0 copy-done
  43.9 0.0 copy-done.1
  43.9 0.0 copy-start.4
  43.9 0.0 copy-start.5
  43.9 4.0 %all-to-all-start.1 = ((bf16[128,48,256]{2,1,0:T(8,128)(2,1)}), bf16[128,48,256]{2,1,0:T(8,128)(2,1)S(1)}, u32[]{:S(2)}, u32[]{:S(2)}) async-start(bf16[128,48,256]{2,1,0:T(8,128)(2,1)} %chosen_rows.1), calls=%async_computation.1 | async-start | bytes 6291456 | tf_op jit(solution)/shard_map/all_to_all | solution.py:22
  47.9 0.0 copy-done.4
  48.0 0.8 copy.32
  48.8 2.2 %select_reduce_fusion = f32[32,16,8]{2,1,0:T(8,128)S(1)} fusion(f32[64]{0:T(128)S(1)} %copy-done.6, s32[32,16,8]{2,1,0:T(8,128)} %copy.32), kind=kLoop, calls=%fused_computation.1 | loop fusion | flops 782336 | bytes 33024 | tf_op jit(solution)/shard_map/reduce_sum | solution.py:31
  51.0 0.2 copy.33
  51.2 0.0 copy-done.5
  51.2 0.8 fusion
  52.1 0.8 select_reduce_fusion.1
  52.8 1.1 copy.34
  53.9 2.6 %copy.35 = f32[512,512]{0,1:T(8,128)} copy(f32[512,512]{1,0:T(8,128)} %param.18) | data formatting | bytes 2097152 | tf_op args[8]
  56.5 2.5 %reshape.41 = f32[512,128,4]{0,2,1:T(4,128)} reshape(f32[512,512]{0,1:T(8,128)} %copy.35) | data formatting | bytes 2097152 | tf_op jit(solution)/shard_map/reshape | solution.py:436
  59.0 2.3 %copy.36 = f32[512,4,128]{2,1,0:T(4,128)} copy(f32[512,4,128]{0,1,2:T(4,128)} %bitcast.36) | data formatting | bytes 2097152 | tf_op jit(solution)/shard_map/transpose | solution.py:436
  61.3 2.2 %copy.43 = f32[64,8,4,128]{3,1,2,0:T(8,128)} copy(f32[64,8,4,128]{3,2,1,0:T(4,128)} %bitcast.37) | data formatting | bytes 2097152
  63.5 2.0 %fusion.1.radial = f32[4,8,16,512]{3,2,1,0:T(8,128)} fusion(f32[4,8,16,16]{3,2,1,0:T(8,128)S(1)} %bitcast.41, f32[16,512]{1,0:T(8,128)S(1)} %copy-done.2), kind=kOutput, calls=%fused_computation.8 | convolution fusion | flops 50331648 | bytes 1114112 | tf_op jit(solution)/shard_map/dot_general | solution.py:38
  65.5 15.5 %assemble_strip.1.blocks = bf16[80,1024,256]{2,1,0:T(8,128)(2,1)} custom-call(bf16[4,8,64,512]{3,2,1,0:T(8,128)(2,1)} %bitcast.39, f32[4,8,16,512]{3,2,1,0:T(8,128)} %fusion.1.radial, bf16[128,40,128]{2,1,0:T(8,128)(2,1)} %copy-done, bf16[128,40,128]{2,1,0:T(8,128)(2,1)} %copy-done.1, f32[512,512]{1,0:T(8,128)} %bitcast.35), custom_call_target="tpu_custom_call" | custom-call | flops 8589934592 | bytes 8388608 | tf_op jit(solution)/shard_map/assemble_strip/pallas_call | solution.py:438
  81.0 8.1 %all-to-all-done.1.got = bf16[128,48,256]{2,1,0:T(8,128)(2,1)S(1)} async-done(((bf16[128,48,256]{2,1,0:T(8,128)(2,1)}), bf16[128,48,256]{2,1,0:T(8,128)(2,1)S(1)}, u32[]{:S(2)}, u32[]{:S(2)}) %all-to-all-start.1) | async-done | bytes 3145760 | tf_op jit(solution)/shard_map/all_to_all | solution.py:22
  89.1 6.1 %update_blocks.1 = (bf16[8,1024,256]{2,1,0:T(8,128)(2,1)S(1)}, bf16[64,512]{1,0:T(8,128)(2,1)}) custom-call(bf16[128,48,256]{2,1,0:T(8,128)(2,1)S(1)} %all-to-all-done.1.got, bf16[80,1024,256]{2,1,0:T(8,128)(2,1)} %assemble_strip.1.blocks), custom_call_target="tpu_custom_call" | custom-call | flops 3758096384 | bytes 12582912 | tf_op jit(solution)/shard_map/update_blocks/pallas_call | solution.py:454
  95.2 57.0 %all_to_all.15.got = bf16[128,64,256]{2,1,0:T(8,128)(2,1)S(1)} all-to-all(bf16[128,64,256]{2,1,0:T(8,128)(2,1)S(1)} %bitcast.33), channel_id=1, replica_groups=mesh['row'=8,'col'=16] {'row','col'}, dimensions={0} | all-to-all | bytes 8388608 | tf_op jit(solution)/shard_map/all_to_all | solution.py:22
  152.2 3.4 %widen_blocks.1 = f32[64,32768]{1,0:T(8,128)} custom-call(bf16[128,64,256]{2,1,0:T(8,128)(2,1)S(1)} %all_to_all.15.got), custom_call_target="tpu_custom_call" | custom-call | flops 2097152 | bytes 12582912 | tf_op jit(solution)/shard_map/widen_blocks/pallas_call | solution.py:478
Async XLA Ops:
  5.0 11.5 %copy-start.3 = (bf16[32,32768]{1,0:T(8,128)(2,1)S(1)}, bf16[32,32768]{1,0:T(8,128)(2,1)}, u32[]{:S(2)}) copy-start(bf16[32,32768]{1,0:T(8,128)(2,1)} %param.19) | copy-start | bytes 6291460
  5.0 32.8 %all-to-all-start = ((bf16[128,40,128]{2,1,0:T(8,128)(2,1)}), bf16[128,40,128]{2,1,0:T(8,128)(2,1)S(1)}, u32[]{:S(2)}, u32[]{:S(2)}) async-start(bf16[128,40,128]{2,1,0:T(8,128)(2,1)} %pick_pivots.1), calls=%async_computation | async-start | bytes 2621440 | tf_op jit(solution)/shard_map/all_to_all | solution.py:22
  16.8 22.5 %copy-start.6 = (f32[64]{0:T(128)S(1)}, f32[64]{0:T(128)}, u32[]{:S(2)}) copy-start(f32[64]{0:T(128)} %param.15) | copy-start | bytes 772
  16.8 22.6 %copy-start.2 = (f32[16,512]{1,0:T(8,128)S(1)}, f32[16,512]{1,0:T(8,128)}, u32[]{:S(2)}) copy-start(f32[16,512]{1,0:T(8,128)} %kernels_at.1) | copy-start | bytes 98308
  37.9 6.0 %copy-start = (bf16[128,40,128]{2,1,0:T(8,128)(2,1)}, bf16[128,40,128]{2,1,0:T(8,128)(2,1)S(1)}, u32[]{:S(2)}) copy-start(bf16[128,40,128]{2,1,0:T(8,128)(2,1)S(1)} %all-to-all-done.got) | copy-start | bytes 3932164
  37.9 4.2 %collective-permute-start = (bf16[128,40,128]{2,1,0:T(8,128)(2,1)S(1)}, bf16[128,40,128]{2,1,0:T(8,128)(2,1)S(1)}, u32[]{:S(2)}, u32[]{:S(2)}) collective-permute-start(bf16[128,40,128]{2,1,0:T(8,128)(2,1)S(1)} %all-to-all-done.got), channel_id=1, source_target_pairs={{0,16},{16,0},{32,48},{48,32},{64,80},{80,64},{96,112},{112,96},{1... | collective-permute-start | bytes 3932168 | tf_op jit(solution)/shard_map/ppermute | solution.py:396
  42.0 1.9 %copy-start.1 = (bf16[128,40,128]{2,1,0:T(8,128)(2,1)}, bf16[128,40,128]{2,1,0:T(8,128)(2,1)S(1)}, u32[]{:S(2)}) copy-start(bf16[128,40,128]{2,1,0:T(8,128)(2,1)S(1)} %collective-permute-done.other) | copy-start | bytes 3932164
  43.9 4.0 %copy-start.4 = (s32[32,16,8]{0,2,1:T(8,128)S(1)}, s32[32,16,8]{0,2,1:T(8,128)}, u32[]{:S(2)}) copy-start(s32[32,16,8]{0,2,1:T(8,128)} %param.13) | copy-start | bytes 49156
  43.9 7.3 %copy-start.5 = (s32[32,16]{0,1:T(8,128)S(1)}, s32[32,16]{0,1:T(8,128)}, u32[]{:S(2)}) copy-start(s32[32,16]{0,1:T(8,128)} %param.14) | copy-start | bytes 6148
  43.9 45.2 %all-to-all-start.1 = ((bf16[128,48,256]{2,1,0:T(8,128)(2,1)}), bf16[128,48,256]{2,1,0:T(8,128)(2,1)S(1)}, u32[]{:S(2)}, u32[]{:S(2)}) async-start(bf16[128,48,256]{2,1,0:T(8,128)(2,1)} %chosen_rows.1), calls=%async_computation.1 | async-start | bytes 6291456 | tf_op jit(solution)/shard_map/all_to_all | solution.py:22

commit v5 on v4

--- a/solution.py
+++ b/solution.py
@@ -216,8 +216,12 @@
     ]
     chosen = jnp.concatenate(chosen, axis=0)
     many, rows, wide = wave.shape
-    tile = jnp.concatenate([chosen[:, at : at + wide] for at in range(0, scols, wide)], axis=0).astype(BF16)
-    wave[...] = jnp.broadcast_to(tile[None], wave.shape)
+    each = many // CORES
+    for core in range(CORES):
+        start = core * (scols // CORES)
+        cuts = [chosen[:, at : at + wide] for at in range(start, start + scols // CORES, wide)]
+        tile = jnp.concatenate(cuts, axis=0).astype(BF16)
+        wave[core * each : (core + 1) * each] = jnp.broadcast_to(tile[None], (each,) + wave.shape[1:])
     sends = []
     for g in range(ndev // many):
         send = pltpu.make_async_copy(
@@ -266,47 +270,60 @@
         send(p).wait()
 
 
-def update_kernel(own, got, blocks, out, upper_t, low1, low2, before, upper_all, spread, chosen, sems, low_sems):
-    npiv, scols = chosen.shape
-    ndev, deep2, wide = got.shape
-    nrow = before.shape[0]
-    ncol = ndev // nrow
-    deep = npiv // ncol
-    rows = deep2 - deep
+def upper_kernel(own, slot, got, blocks, upper, low1, low2, spread, chosen, low_sems):
+    npiv, half = chosen.shape
+    ndev, rows, lanes = got.shape[0], spread.shape[0] // got.shape[0], got.shape[2]
+    wide = blocks.shape[2]
     lows = []
     for i, low in enumerate((low1, low2)):
         for h in range(npiv // wide):
             lows.append(
                 pltpu.make_async_copy(
-                    blocks.at[nrow + i, pl.ds(h * npiv, npiv), :], low.at[:, pl.ds(h * wide, wide)], low_sems.at[i, h]
+                    blocks.at[slot + i, pl.ds(h * npiv, npiv), :], low.at[:, pl.ds(h * wide, wide)], low_sems.at[i, h]
                 )
             )
-    loads = [pltpu.make_async_copy(blocks.at[p], before.at[p], sems.at[p]) for p in range(nrow)]
-    for load in lows + loads:
+    for load in lows:
         load.start()
-    for b in range(wide // LANES):
-        spread[b] = got[:, deep:, b * LANES : (b + 1) * LANES].astype(F32).reshape(ndev * rows, LANES)
-        for h in range(scols // wide):
-            start = h * wide + b * LANES
-            for a in range(own):
-                chosen[a * ndev : (a + 1) * ndev, start : start + LANES] = spread[
-                    b, pl.ds(h * own + a, ndev, stride=rows), :
-                ].astype(BF16)
+    spread[...] = got[:, got.shape[1] - rows :, :].astype(F32).reshape(ndev * rows, lanes)
+    for g in range(half // lanes):
+        for a in range(own):
+            chosen[a * ndev : (a + 1) * ndev, g * lanes : (g + 1) * lanes] = spread[
+                pl.ds(g * own + a, ndev, stride=rows), :
+            ].astype(BF16)
     for load in lows:
         load.wait()
-    for at in range(0, scols, wide):
+    for at in range(0, half, wide):
         rows_of = chosen[:, at : at + wide]
-        upper = jnp.dot(low1[...], rows_of, preferred_element_type=F32) + jnp.dot(
+        part = jnp.dot(low1[...], rows_of, preferred_element_type=F32) + jnp.dot(
             low2[...], rows_of, preferred_element_type=F32
         )
-        upper_all[at : at + wide, :] = upper.T.astype(BF16)
+        upper[at : at + wide, :] = part.T.astype(BF16)
+
+
+def fetch_kernel(blocks, upper, out, sems):
+    del upper
+    loads = [pltpu.make_async_copy(blocks.at[p], out.at[p], sems.at[p]) for p in range(out.shape[0])]
+    for load in loads:
+        load.start()
+    for load in loads:
+        load.wait()
+
+
+def update_kernel(deep, got, mine, theirs, before, out, upper_t, upper_all):
+    nrow, scols, wide = before.shape
+    half, npiv = mine.shape
+    ncol = npiv // deep
+    core = lax.rem(lax.axis_index("row"), CORES)
+    upper_all[pl.ds(pl.multiple_of(core * half, half), half), :] = mine[...]
+    upper_all[pl.ds(pl.multiple_of((1 - core) * half, half), half), :] = theirs[...]
     width = upper_t.shape[0]
     upper_t[...] = upper_all[pl.ds(pl.multiple_of(lax.axis_index("col") * width, width), width), :]
-    for load in loads:
-        load.wait()
     for p in range(nrow):
-        columns = got[p * ncol : (p + 1) * ncol, :deep, :].reshape(npiv, wide)
-        change = jnp.dot(upper_all[...], columns, preferred_element_type=F32)
+        pieces = [
+            got[p * ncol : (p + 1) * ncol, b * deep : (b + 1) * deep, :].reshape(npiv, LANES)
+            for b in range(wide // LANES)
+        ]
+        change = jnp.dot(upper_all[...], jnp.concatenate(pieces, axis=1), preferred_element_type=F32)
         out[p] = (before[p].astype(F32) - change).astype(BF16)
 
 
@@ -388,8 +405,10 @@
         form_strip,
     )
     deep, wide = panel.shape[0], panel.shape[1] // ndev
-    cut = panel.reshape(deep, ndev, wide).transpose(1, 0, 2)
-    wave_rows = own * scols // wide
+    flat = deep * wide // LANES
+    cut = panel.reshape(deep, ndev, wide // LANES, LANES).transpose(1, 2, 0, 3).reshape(ndev, flat, LANES)
+    half = scols // CORES
+    wave_rows = own * half // LANES
     second = jnp.pad(cut, ((0, 0), (0, wave_rows), (0, 0)))
     got = exchange(first)
     got, second = lax.optimization_barrier((got, second))
@@ -418,7 +437,7 @@
         out_specs=anywhere,
         scratch_shapes=[
             pltpu.VMEM((nstrip, nmom, nrad), BF16),
-            pltpu.VMEM((many, wave_rows, wide), BF16),
+            pltpu.VMEM((many, wave_rows, LANES), BF16),
             dma((CORES * nrow,)),
             dma((ndev // many,)),
         ],
@@ -451,28 +470,46 @@
         name="assemble_strip",
     )(form_rows.reshape(group, nrow, nmom, nrad), radial.reshape(group, nrow, nstrip, nrad), got, other, lower)
 
+    mine = pl.pallas_call(
+        functools.partial(upper_kernel, own, nrow),
+        out_shape=jax.ShapeDtypeStruct((half, npiv), BF16),
+        in_specs=[vmem, anywhere],
+        out_specs=vmem,
+        scratch_shapes=[
+            pltpu.VMEM((npiv, npiv), BF16),
+            pltpu.VMEM((npiv, npiv), BF16),
+            pltpu.VMEM((ndev * wave_rows, LANES), F32),
+            pltpu.VMEM((npiv, half), BF16),
+            dma((2, npiv // wide)),
+        ],
+        compiler_params=room(24),
+        cost_estimate=cost(4 * npiv * npiv * half, 2 << 20),
+        name="upper_rows",
+    )(got2, blocks)
+    theirs = lax.ppermute(mine, "row", [(i, i ^ 1) for i in range(nrow)])
+    fetched = pl.pallas_call(
+        fetch_kernel,
+        out_shape=jax.ShapeDtypeStruct((nrow, scols, wide), BF16),
+        in_specs=[anywhere, anywhere],
+        out_specs=vmem,
+        scratch_shapes=[dma((nrow,))],
+        compiler_params=room(16),
+        cost_estimate=cost(0, 8 << 20),
+        name="fetch_blocks",
+    )(blocks, mine)
     done, upper_t = pl.pallas_call(
-        functools.partial(update_kernel, own),
+        functools.partial(update_kernel, deep),
         out_shape=(
             jax.ShapeDtypeStruct((nrow, scols, wide), BF16),
             jax.ShapeDtypeStruct((width, npiv), BF16),
         ),
-        in_specs=[vmem, anywhere],
+        in_specs=[vmem, vmem, vmem, vmem],
         out_specs=(vmem, vmem),
-        scratch_shapes=[
-            pltpu.VMEM((npiv, npiv), BF16),
-            pltpu.VMEM((npiv, npiv), BF16),
-            pltpu.VMEM((nrow, scols, wide), BF16),
-            pltpu.VMEM((scols, npiv), BF16),
-            pltpu.VMEM((wide // LANES, ndev * wave_rows, LANES), F32),
-            pltpu.VMEM((npiv, scols), BF16),
-            dma((nrow,)),
-            dma((2, npiv // wide)),
-        ],
-        compiler_params=room(24),
-        cost_estimate=cost(2 * npiv * scols * (3 * npiv + local), 12 << 20),
+        scratch_shapes=[pltpu.VMEM((scols, npiv), BF16)],
+        compiler_params=room(16),
+        cost_estimate=cost(2 * npiv * scols * local, 12 << 20),
         name="update_blocks",
-    )(got2, blocks)
+    )(got2, mine, theirs, fetched)
     final = exchange(done.reshape(ndev, width, wide))
     steps = 16
     trailing = pl.pallas_call(

time: 156 us -> 152 us (0.974)
  waiting for transfers between devices: 28.8 us -> 21.9 us
  local copies, waits for them, and re-layouts: 14 us -> 17.6 us
  other arithmetic: 3.88 us -> 1.49 us
    all_to_all x2, waiting for transfers between devices: 27.3 us -> 20.3 us  [exchange(): return lax.all_to_all(chunks, ALL, split_axis=0, concat_axis=0, tiled=True)]
    reshape x1 -> x2, local copies, waits for them, and re-layouts: 0.28 us -> 5.68 us  [shards(): panel.reshape(deep, ndev, wide // LANES, LANES).transpose(1, 2, 0, 3)]
    pallas_call x1 -> x3, Pallas kernels: 6.11 us -> 7.16 us  [the longest x1 2.91 us: shards(): pl.pallas_call(functools.partial(update_kernel, deep), out_shape=(jax.Sha...]
  transfers between devices with their start and end apart: 3 -> 4, of which waited for: 3 -> 3; matrix products, arithmetic and copies ran while one was open for 13% -> 14% of each run, Pallas kernels for 11% -> 12%
where the time goes in v5:
time: 152 us; the launch traced here: 151 us
  blocking collectives  56.2 us (37%)
  Pallas kernels  33.1 us (22%)
  waiting for transfers between devices  21.9 us (14%)
  starting transfers between devices  17.9 us (12%)
  local copies, waits for them, and re-layouts  17.6 us (12%)
  matrix products  1.96 us (1%)
    all_to_all x1, blocking collectives, exchange(): return lax.all_to_all(chunks, ALL, split_axis=0, concat_axis=0, tiled=True)  56.2 us
    all_to_all x2, waiting for transfers between devices, exchange(): return lax.all_to_all(chunks, ALL, split_axis=0, concat_axis=0, tiled=True)  20.3 us
    pallas_call x1, Pallas kernels, shards(): pl.pallas_call(assemble_kernel, out_shape=jax.ShapeDtypeStruct((slots, sc...  15.5 us
    all_to_all x2, starting transfers between devices, exchange(): return lax.all_to_all(chunks, ALL, split_axis=0, concat_axis=0, tiled=True)  15.5 us
    reshape x2, local copies, waits for them, and re-layouts, shards(): panel.reshape(deep, ndev, wide // LANES, LANES).transpose(1, 2, 0, 3)  5.68 us
    unnamed x17, local copies, waits for them, and re-layouts  5.04 us
    pallas_call x1, Pallas kernels, shards(): pl.pallas_call(functools.partial(pick_kernel, own), out_shape=jax.ShapeDt...  4.35 us
    pallas_call x1, Pallas kernels, shards(): pl.pallas_call(widen_kernel, out_shape=jax.ShapeDtypeStruct((width, ndev...  3.45 us
  transfers between devices with their start and end apart: 4, of which 3 were waited for; matrix products, arithmetic and copies ran while one was open for 14% of the time, Pallas kernels for 12%

profile of v5, /device:TPU:1, one launch (start us, length us, event | category | flops | bytes accessed | tf_op | source)
XLA Modules:
  0.0 151.2 jit_solution(13606814338630756201)
XLA Ops:
  0.6 4.4 %pick_pivots.1 = bf16[128,40,128]{2,1,0:T(8,128)(2,1)} custom-call(s32[1,512]{1,0:T(1,128)} %bitcast.41, s32[128,32]{1,0:T(8,128)} %bitcast.38, s32[128,32]{1,0:T(8,128)} %bitcast.37, s32[16,32]{1,0:T(8,128)} %bitcast.39, bf16[2048,512]{1,0:T(8,128)(2,1)} %bitcast.34, bf16[1,64,512]{2,1,0:T(8,128)(2,1)} %form_strip_at.1), custom_call_target="tpu_custom_call" | custom-call | flops 1073741824 | bytes 4194304 | tf_op jit(solution)/shard_map/pick_pivots/pallas_call | solution.py:378
  5.0 11.5 %all-to-all-start = ((bf16[128,40,128]{2,1,0:T(8,128)(2,1)}), bf16[128,40,128]{2,1,0:T(8,128)(2,1)S(1)}, u32[]{:S(2)}, u32[]{:S(2)}) async-start(bf16[128,40,128]{2,1,0:T(8,128)(2,1)} %pick_pivots.1), calls=%async_computation | async-start | bytes 2621440 | tf_op jit(solution)/shard_map/all_to_all | solution.py:22
  16.5 3.2 %reshape.42 = bf16[32,128,2,128]{3,2,1,0:T(2,128)(2,1)S(1)} reshape(bf16[32,32768]{1,0:T(8,128)(2,1)} %param.19) | data formatting | bytes 4194304 | tf_op jit(solution)/shard_map/reshape | solution.py:409
  19.8 2.4 %copy.31 = bf16[32,128,2,128]{3,0,2,1:T(8,128)(2,1)S(1)} copy(bf16[32,128,2,128]{3,2,1,0:T(2,128)(2,1)S(1)} %reshape.42) | data formatting | bytes 4194304 | tf_op jit(solution)/shard_map/reshape | solution.py:409
  22.2 0.0 copy-start.6
  22.2 0.0 copy-start.2
  22.2 1.7 %pad.4.kept = bf16[128,80,128]{2,1,0:T(8,128)(2,1)} pad(bf16[128,64,128]{2,1,0:T(8,128)(2,1)S(1)} %bitcast.30, bf16[]{:T(256)} %constant.6.clone.1), padding=0_0x0_16x0_0 | pad | bytes 4718594 | tf_op jit(solution)/shard_map/jit(_pad)/pad | solution.py:412
  23.9 13.9 %all-to-all-done.got = bf16[128,40,128]{2,1,0:T(8,128)(2,1)S(1)} async-done(((bf16[128,40,128]{2,1,0:T(8,128)(2,1)}), bf16[128,40,128]{2,1,0:T(8,128)(2,1)S(1)}, u32[]{:S(2)}, u32[]{:S(2)}) %all-to-all-start) | async-done | bytes 1310752 | tf_op jit(solution)/shard_map/all_to_all | solution.py:22
  37.8 0.0 copy-start
  37.8 1.5 collective-permute-start
  39.3 0.0 copy-done.6
  39.3 0.1 copy.32.angular_at
  39.4 0.0 copy-done.2
  39.4 1.0 scale_pivots.1.scaled
  40.4 1.6 %collective-permute-done.other = bf16[128,40,128]{2,1,0:T(8,128)(2,1)S(1)} collective-permute-done((bf16[128,40,128]{2,1,0:T(8,128)(2,1)S(1)}, bf16[128,40,128]{2,1,0:T(8,128)(2,1)S(1)}, u32[]{:S(2)}, u32[]{:S(2)}) %collective-permute-start) | collective-permute-done | bytes 1310752 | tf_op jit(solution)/shard_map/ppermute | solution.py:415
  42.0 0.0 copy-start.1
  42.0 1.7 %chosen_rows.1 = bf16[128,80,128]{2,1,0:T(8,128)(2,1)} custom-call(bf16[128,40,128]{2,1,0:T(8,128)(2,1)S(1)} %all-to-all-done.got, bf16[128,40,128]{2,1,0:T(8,128)(2,1)S(1)} %collective-permute-done.other, bf16[64,512]{1,0:T(8,128)(2,1)S(1)} %scale_pivots.1.scaled, bf16[128,80,128]{2,1,0:T(8,128)(2,1)} %pad.4.kept), custom_call_target="tpu_custom_call", output_to_operand_aliasing={{}: (3, {})} | custom-call | flops 67108864 | bytes 4194304 | tf_op jit(solution)/shard_map/chosen_rows/pallas_call | solution.py:433
  43.7 0.0 copy-done
  43.7 0.0 copy-done.1
  43.7 0.0 copy-start.3
  43.7 0.0 copy-start.4
  43.7 0.0 copy-start.5
  43.8 4.0 %all-to-all-start.1 = ((bf16[128,80,128]{2,1,0:T(8,128)(2,1)}), bf16[128,80,128]{2,1,0:T(8,128)(2,1)S(1)}, u32[]{:S(2)}, u32[]{:S(2)}) async-start(bf16[128,80,128]{2,1,0:T(8,128)(2,1)} %chosen_rows.1), calls=%async_computation.1 | async-start | bytes 5242880 | tf_op jit(solution)/shard_map/all_to_all | solution.py:22
  47.8 0.0 copy-done.3
  47.8 0.2 copy.33
  47.9 1.3 select_reduce_fusion
  49.3 0.2 copy.34
  49.4 0.0 copy-done.4
  49.4 0.0 copy-done.5
  49.5 0.1 select_reduce_fusion.1
  49.6 0.2 copy.35
  49.8 2.6 %copy.36 = f32[512,512]{0,1:T(8,128)} copy(f32[512,512]{1,0:T(8,128)} %param.18) | data formatting | bytes 2097152 | tf_op args[8]
  52.4 2.5 %reshape.45 = f32[512,128,4]{0,2,1:T(4,128)} reshape(f32[512,512]{0,1:T(8,128)} %copy.36) | data formatting | bytes 2097152 | tf_op jit(solution)/shard_map/reshape | solution.py:455
  54.9 2.3 %copy.37 = f32[512,4,128]{2,1,0:T(4,128)} copy(f32[512,4,128]{0,1,2:T(4,128)} %bitcast.32) | data formatting | bytes 2097152 | tf_op jit(solution)/shard_map/transpose | solution.py:455
  57.1 2.2 %copy.41 = f32[64,8,4,128]{3,1,2,0:T(8,128)} copy(f32[64,8,4,128]{3,2,1,0:T(4,128)} %bitcast.33) | data formatting | bytes 2097152
  59.4 2.0 %fusion.1.radial = f32[4,8,16,512]{3,2,1,0:T(8,128)} fusion(f32[4,8,16,16]{3,2,1,0:T(8,128)S(1)} %bitcast.36, f32[16,512]{1,0:T(8,128)S(1)} %copy-done.2), kind=kOutput, calls=%fused_computation.7 | convolution fusion | flops 50331648 | bytes 1114112 | tf_op jit(solution)/shard_map/dot_general | solution.py:38
  61.3 15.5 %assemble_strip.1.blocks = bf16[80,1024,256]{2,1,0:T(8,128)(2,1)} custom-call(bf16[4,8,64,512]{3,2,1,0:T(8,128)(2,1)} %bitcast.35, f32[4,8,16,512]{3,2,1,0:T(8,128)} %fusion.1.radial, bf16[128,40,128]{2,1,0:T(8,128)(2,1)} %copy-done, bf16[128,40,128]{2,1,0:T(8,128)(2,1)} %copy-done.1, f32[512,512]{1,0:T(8,128)} %bitcast.31), custom_call_target="tpu_custom_call" | custom-call | flops 8589934592 | bytes 8388608 | tf_op jit(solution)/shard_map/assemble_strip/pallas_call | solution.py:457
  76.8 6.4 %all-to-all-done.1.got = bf16[128,80,128]{2,1,0:T(8,128)(2,1)S(1)} async-done(((bf16[128,80,128]{2,1,0:T(8,128)(2,1)}), bf16[128,80,128]{2,1,0:T(8,128)(2,1)S(1)}, u32[]{:S(2)}, u32[]{:S(2)}) %all-to-all-start.1) | async-done | bytes 2621472 | tf_op jit(solution)/shard_map/all_to_all | solution.py:22
  83.3 2.0 %upper_rows.1.upper.mine = bf16[512,512]{1,0:T(8,128)(2,1)S(1)} custom-call(bf16[128,80,128]{2,1,0:T(8,128)(2,1)S(1)} %all-to-all-done.1.got, bf16[80,1024,256]{2,1,0:T(8,128)(2,1)} %assemble_strip.1.blocks), custom_call_target="tpu_custom_call" | custom-call | flops 536870912 | bytes 2097152 | tf_op jit(solution)/shard_map/upper_rows/pallas_call | solution.py:473
  85.3 0.9 collective-permute-start.1
  86.3 2.2 %fetch_blocks.1.before = bf16[8,1024,256]{2,1,0:T(8,128)(2,1)S(1)} custom-call(bf16[80,1024,256]{2,1,0:T(8,128)(2,1)} %assemble_strip.1.blocks, bf16[512,512]{1,0:T(8,128)(2,1)S(1)} %upper_rows.1.upper.mine), custom_call_target="tpu_custom_call" | custom-call | bytes 8388608 | tf_op jit(solution)/shard_map/fetch_blocks/pallas_call | solution.py:490
  88.5 0.0 collective-permute-done.1.theirs
  88.5 2.9 %update_blocks.1 = (bf16[8,1024,256]{2,1,0:T(8,128)(2,1)S(1)}, bf16[64,512]{1,0:T(8,128)(2,1)}) custom-call(bf16[128,80,128]{2,1,0:T(8,128)(2,1)S(1)} %all-to-all-done.1.got, bf16[512,512]{1,0:T(8,128)(2,1)S(1)} %upper_rows.1.upper.mine, bf16[512,512]{1,0:T(8,128)(2,1)S(1)} %collective-permute-done.1.theirs, bf16[8,1024,256]{2,1,0:T(8,128)(2,1)S(1)} %fetch_blocks.1.before), custom_call_target="tpu_custom_call" | custom-call | flops 2147483648 | bytes 12582912 | tf_op jit(solution)/shard_map/update_blocks/pallas_call | solution.py:500
  91.4 56.2 %all_to_all.15.got = bf16[128,64,256]{2,1,0:T(8,128)(2,1)S(1)} all-to-all(bf16[128,64,256]{2,1,0:T(8,128)(2,1)S(1)} %bitcast.29), channel_id=1, replica_groups=mesh['row'=8,'col'=16] {'row','col'}, dimensions={0} | all-to-all | bytes 8388608 | tf_op jit(solution)/shard_map/all_to_all | solution.py:22
  147.6 3.4 %widen_blocks.1 = f32[64,32768]{1,0:T(8,128)} custom-call(bf16[128,64,256]{2,1,0:T(8,128)(2,1)S(1)} %all_to_all.15.got), custom_call_target="tpu_custom_call" | custom-call | flops 2097152 | bytes 12582912 | tf_op jit(solution)/shard_map/widen_blocks/pallas_call | solution.py:515
  (1 shorter events, 0.0 us)
Async XLA Ops:
  5.0 32.8 %all-to-all-start = ((bf16[128,40,128]{2,1,0:T(8,128)(2,1)}), bf16[128,40,128]{2,1,0:T(8,128)(2,1)S(1)}, u32[]{:S(2)}, u32[]{:S(2)}) async-start(bf16[128,40,128]{2,1,0:T(8,128)(2,1)} %pick_pivots.1), calls=%async_computation | async-start | bytes 2621440 | tf_op jit(solution)/shard_map/all_to_all | solution.py:22
  22.2 17.2 %copy-start.6 = (f32[64]{0:T(128)S(1)}, f32[64]{0:T(128)}, u32[]{:S(2)}) copy-start(f32[64]{0:T(128)} %param.15) | copy-start | bytes 772
  22.2 17.2 %copy-start.2 = (f32[16,512]{1,0:T(8,128)S(1)}, f32[16,512]{1,0:T(8,128)}, u32[]{:S(2)}) copy-start(f32[16,512]{1,0:T(8,128)} %kernels_at.1) | copy-start | bytes 98308
  37.8 5.9 %copy-start = (bf16[128,40,128]{2,1,0:T(8,128)(2,1)}, bf16[128,40,128]{2,1,0:T(8,128)(2,1)S(1)}, u32[]{:S(2)}) copy-start(bf16[128,40,128]{2,1,0:T(8,128)(2,1)S(1)} %all-to-all-done.got) | copy-start | bytes 3932164
  37.8 4.2 %collective-permute-start = (bf16[128,40,128]{2,1,0:T(8,128)(2,1)S(1)}, bf16[128,40,128]{2,1,0:T(8,128)(2,1)S(1)}, u32[]{:S(2)}, u32[]{:S(2)}) collective-permute-start(bf16[128,40,128]{2,1,0:T(8,128)(2,1)S(1)} %all-to-all-done.got), channel_id=1, source_target_pairs={{0,16},{16,0},{32,48},{48,32},{64,80},{80,64},{96,112},{112,96},{1... | collective-permute-start | bytes 3932168 | tf_op jit(solution)/shard_map/ppermute | solution.py:415
  42.0 1.7 %copy-start.1 = (bf16[128,40,128]{2,1,0:T(8,128)(2,1)}, bf16[128,40,128]{2,1,0:T(8,128)(2,1)S(1)}, u32[]{:S(2)}) copy-start(bf16[128,40,128]{2,1,0:T(8,128)(2,1)S(1)} %collective-permute-done.other) | copy-start | bytes 3932164
  43.7 4.0 %copy-start.3 = (s32[32,16,8]{0,2,1:T(8,128)S(1)}, s32[32,16,8]{0,2,1:T(8,128)}, u32[]{:S(2)}) copy-start(s32[32,16,8]{0,2,1:T(8,128)} %param.13) | copy-start | bytes 49156
  43.7 5.7 %copy-start.4 = (s32[32,16,8]{0,2,1:T(8,128)S(1)}, s32[32,16,8]{0,2,1:T(8,128)}, u32[]{:S(2)}) copy-start(s32[32,16,8]{0,2,1:T(8,128)} %param.12) | copy-start | bytes 49156
  43.7 5.7 %copy-start.5 = (s32[32,16]{0,1:T(8,128)S(1)}, s32[32,16]{0,1:T(8,128)}, u32[]{:S(2)}) copy-start(s32[32,16]{0,1:T(8,128)} %param.14) | copy-start | bytes 6148
  43.8 39.5 %all-to-all-start.1 = ((bf16[128,80,128]{2,1,0:T(8,128)(2,1)}), bf16[128,80,128]{2,1,0:T(8,128)(2,1)S(1)}, u32[]{:S(2)}, u32[]{:S(2)}) async-start(bf16[128,80,128]{2,1,0:T(8,128)(2,1)} %chosen_rows.1), calls=%async_computation.1 | async-start | bytes 5242880 | tf_op jit(solution)/shard_map/all_to_all | solution.py:22
  85.3 3.2 %collective-permute-start.1 = (bf16[512,512]{1,0:T(8,128)(2,1)S(1)}, bf16[512,512]{1,0:T(8,128)(2,1)S(1)}, u32[]{:S(2)}, u32[]{:S(2)}) collective-permute-start(bf16[512,512]{1,0:T(8,128)(2,1)S(1)} %upper_rows.1.upper.mine), channel_id=1, source_target_pairs={{0,16},{16,0},{32,48},{48,32},{64,80},{80,64},{96,112},{112,96},{1... | collective-permute-start | bytes 1572872 | tf_op jit(solution)/shard_map/ppermute | solution.py:489

commit v6 on v5

--- a/solution.py
+++ b/solution.py
@@ -290,14 +290,18 @@
             chosen[a * ndev : (a + 1) * ndev, g * lanes : (g + 1) * lanes] = spread[
                 pl.ds(g * own + a, ndev, stride=rows), :
             ].astype(BF16)
-    for load in lows:
+    each = npiv // wide
+    for load in lows[:each]:
         load.wait()
-    for at in range(0, half, wide):
-        rows_of = chosen[:, at : at + wide]
-        part = jnp.dot(low1[...], rows_of, preferred_element_type=F32) + jnp.dot(
-            low2[...], rows_of, preferred_element_type=F32
-        )
-        upper[at : at + wide, :] = part.T.astype(BF16)
+    parts = [
+        jnp.dot(low1[...], chosen[:, at : at + wide], preferred_element_type=F32) for at in range(0, half, wide)
+    ]
+    for load in lows[each:]:
+        load.wait()
+    for i, part in enumerate(parts):
+        span = slice(i * wide, (i + 1) * wide)
+        part = part + jnp.dot(low2[...], chosen[:, span], preferred_element_type=F32)
+        upper[span, :] = part.T.astype(BF16)
 
 
 def fetch_kernel(blocks, upper, out, sems):
@@ -374,7 +378,7 @@
     tall = nmom // (CORES * CORES)
     extra = 2 * nstrip * terms
     deep1 = tall + own * (nrad + extra) // LANES
-    steps, groups = 4, 4
+    steps, groups = 2, 4
     first = pl.pallas_call(
         functools.partial(pick_kernel, own),
         out_shape=jax.ShapeDtypeStruct((ndev, deep1, LANES), BF16),
@@ -511,7 +515,7 @@
         name="update_blocks",
     )(got2, mine, theirs, fetched)
     final = exchange(done.reshape(ndev, width, wide))
-    steps = 16
+    steps = 8
     trailing = pl.pallas_call(
         widen_kernel,
         out_shape=jax.ShapeDtypeStruct((width, ndev * wide), F32),

time: 152 us -> 152 us (level)
  no operation moved by 1% of the time
where the time goes in v6:
time: 152 us; the launch traced here: 151 us
  blocking collectives  56.2 us (37%)
  Pallas kernels  33 us (22%)
  waiting for transfers between devices  21.9 us (14%)
  starting transfers between devices  17.9 us (12%)
  local copies, waits for them, and re-layouts  17.6 us (12%)
  matrix products  1.96 us (1%)
    all_to_all x1, blocking collectives, exchange(): return lax.all_to_all(chunks, ALL, split_axis=0, concat_axis=0, tiled=True)  56.2 us
    all_to_all x2, waiting for transfers between devices, exchange(): return lax.all_to_all(chunks, ALL, split_axis=0, concat_axis=0, tiled=True)  20.3 us
    pallas_call x1, Pallas kernels, shards(): pl.pallas_call(assemble_kernel, out_shape=jax.ShapeDtypeStruct((slots, sc...  15.5 us
    all_to_all x2, starting transfers between devices, exchange(): return lax.all_to_all(chunks, ALL, split_axis=0, concat_axis=0, tiled=True)  15.5 us
    reshape x2, local copies, waits for them, and re-layouts, shards(): panel.reshape(deep, ndev, wide // LANES, LANES).transpose(1, 2, 0, 3)  5.68 us
    unnamed x17, local copies, waits for them, and re-layouts  5.04 us
    pallas_call x1, Pallas kernels, shards(): pl.pallas_call(functools.partial(pick_kernel, own), out_shape=jax.ShapeDt...  4.3 us
    pallas_call x1, Pallas kernels, shards(): pl.pallas_call(widen_kernel, out_shape=jax.ShapeDtypeStruct((width, ndev...  3.43 us
  transfers between devices with their start and end apart: 4, of which 3 were waited for; matrix products, arithmetic and copies ran while one was open for 14% of the time, Pallas kernels for 12%

profile of v6, /device:TPU:1, one launch (start us, length us, event | category | flops | bytes accessed | tf_op | source)
XLA Modules:
  0.0 151.1 jit_solution(1462079456864025302)
XLA Ops:
  0.6 4.3 %pick_pivots.1 = bf16[128,40,128]{2,1,0:T(8,128)(2,1)} custom-call(s32[1,512]{1,0:T(1,128)} %bitcast.41, s32[128,32]{1,0:T(8,128)} %bitcast.38, s32[128,32]{1,0:T(8,128)} %bitcast.37, s32[16,32]{1,0:T(8,128)} %bitcast.39, bf16[2048,512]{1,0:T(8,128)(2,1)} %bitcast.34, bf16[1,64,512]{2,1,0:T(8,128)(2,1)} %form_strip_at.1), custom_call_target="tpu_custom_call" | custom-call | flops 1073741824 | bytes 4194304 | tf_op jit(solution)/shard_map/pick_pivots/pallas_call | solution.py:382
  4.9 11.5 %all-to-all-start = ((bf16[128,40,128]{2,1,0:T(8,128)(2,1)}), bf16[128,40,128]{2,1,0:T(8,128)(2,1)S(1)}, u32[]{:S(2)}, u32[]{:S(2)}) async-start(bf16[128,40,128]{2,1,0:T(8,128)(2,1)} %pick_pivots.1), calls=%async_computation | async-start | bytes 2621440 | tf_op jit(solution)/shard_map/all_to_all | solution.py:22
  16.4 3.2 %reshape.42 = bf16[32,128,2,128]{3,2,1,0:T(2,128)(2,1)S(1)} reshape(bf16[32,32768]{1,0:T(8,128)(2,1)} %param.19) | data formatting | bytes 4194304 | tf_op jit(solution)/shard_map/reshape | solution.py:413
  19.7 2.4 %copy.31 = bf16[32,128,2,128]{3,0,2,1:T(8,128)(2,1)S(1)} copy(bf16[32,128,2,128]{3,2,1,0:T(2,128)(2,1)S(1)} %reshape.42) | data formatting | bytes 4194304 | tf_op jit(solution)/shard_map/reshape | solution.py:413
  22.1 0.0 copy-start.6
  22.2 0.0 copy-start.2
  22.2 1.7 %pad.4.kept = bf16[128,80,128]{2,1,0:T(8,128)(2,1)} pad(bf16[128,64,128]{2,1,0:T(8,128)(2,1)S(1)} %bitcast.30, bf16[]{:T(256)} %constant.6.clone.1), padding=0_0x0_16x0_0 | pad | bytes 4718594 | tf_op jit(solution)/shard_map/jit(_pad)/pad | solution.py:416
  23.9 13.9 %all-to-all-done.got = bf16[128,40,128]{2,1,0:T(8,128)(2,1)S(1)} async-done(((bf16[128,40,128]{2,1,0:T(8,128)(2,1)}), bf16[128,40,128]{2,1,0:T(8,128)(2,1)S(1)}, u32[]{:S(2)}, u32[]{:S(2)}) %all-to-all-start) | async-done | bytes 1310752 | tf_op jit(solution)/shard_map/all_to_all | solution.py:22
  37.8 0.0 copy-start
  37.8 1.5 collective-permute-start
  39.3 0.0 copy-done.6
  39.3 0.1 copy.32.angular_at
  39.4 0.0 copy-done.2
  39.4 1.0 scale_pivots.1.scaled
  40.4 1.6 %collective-permute-done.other = bf16[128,40,128]{2,1,0:T(8,128)(2,1)S(1)} collective-permute-done((bf16[128,40,128]{2,1,0:T(8,128)(2,1)S(1)}, bf16[128,40,128]{2,1,0:T(8,128)(2,1)S(1)}, u32[]{:S(2)}, u32[]{:S(2)}) %collective-permute-start) | collective-permute-done | bytes 1310752 | tf_op jit(solution)/shard_map/ppermute | solution.py:419
  42.0 0.0 copy-start.1
  42.0 1.7 %chosen_rows.1 = bf16[128,80,128]{2,1,0:T(8,128)(2,1)} custom-call(bf16[128,40,128]{2,1,0:T(8,128)(2,1)S(1)} %all-to-all-done.got, bf16[128,40,128]{2,1,0:T(8,128)(2,1)S(1)} %collective-permute-done.other, bf16[64,512]{1,0:T(8,128)(2,1)S(1)} %scale_pivots.1.scaled, bf16[128,80,128]{2,1,0:T(8,128)(2,1)} %pad.4.kept), custom_call_target="tpu_custom_call", output_to_operand_aliasing={{}: (3, {})} | custom-call | flops 67108864 | bytes 4194304 | tf_op jit(solution)/shard_map/chosen_rows/pallas_call | solution.py:437
  43.7 0.0 copy-done
  43.7 0.0 copy-done.1
  43.7 0.0 copy-start.3
  43.7 0.0 copy-start.4
  43.7 0.0 copy-start.5
  43.7 4.0 %all-to-all-start.1 = ((bf16[128,80,128]{2,1,0:T(8,128)(2,1)}), bf16[128,80,128]{2,1,0:T(8,128)(2,1)S(1)}, u32[]{:S(2)}, u32[]{:S(2)}) async-start(bf16[128,80,128]{2,1,0:T(8,128)(2,1)} %chosen_rows.1), calls=%async_computation.1 | async-start | bytes 5242880 | tf_op jit(solution)/shard_map/all_to_all | solution.py:22
  47.7 0.0 copy-done.3
  47.7 0.2 copy.33
  47.9 1.3 select_reduce_fusion
  49.2 0.2 copy.34
  49.4 0.0 copy-done.4
  49.4 0.0 copy-done.5
  49.4 0.1 select_reduce_fusion.1
  49.6 0.2 copy.35
  49.7 2.6 %copy.36 = f32[512,512]{0,1:T(8,128)} copy(f32[512,512]{1,0:T(8,128)} %param.18) | data formatting | bytes 2097152 | tf_op args[8]
  52.3 2.5 %reshape.45 = f32[512,128,4]{0,2,1:T(4,128)} reshape(f32[512,512]{0,1:T(8,128)} %copy.36) | data formatting | bytes 2097152 | tf_op jit(solution)/shard_map/reshape | solution.py:459
  54.8 2.3 %copy.37 = f32[512,4,128]{2,1,0:T(4,128)} copy(f32[512,4,128]{0,1,2:T(4,128)} %bitcast.32) | data formatting | bytes 2097152 | tf_op jit(solution)/shard_map/transpose | solution.py:459
  57.1 2.2 %copy.41 = f32[64,8,4,128]{3,1,2,0:T(8,128)} copy(f32[64,8,4,128]{3,2,1,0:T(4,128)} %bitcast.33) | data formatting | bytes 2097152
  59.3 2.0 %fusion.1.radial = f32[4,8,16,512]{3,2,1,0:T(8,128)} fusion(f32[4,8,16,16]{3,2,1,0:T(8,128)S(1)} %bitcast.36, f32[16,512]{1,0:T(8,128)S(1)} %copy-done.2), kind=kOutput, calls=%fused_computation.7 | convolution fusion | flops 50331648 | bytes 1114112 | tf_op jit(solution)/shard_map/dot_general | solution.py:38
  61.3 15.5 %assemble_strip.1.blocks = bf16[80,1024,256]{2,1,0:T(8,128)(2,1)} custom-call(bf16[4,8,64,512]{3,2,1,0:T(8,128)(2,1)} %bitcast.35, f32[4,8,16,512]{3,2,1,0:T(8,128)} %fusion.1.radial, bf16[128,40,128]{2,1,0:T(8,128)(2,1)} %copy-done, bf16[128,40,128]{2,1,0:T(8,128)(2,1)} %copy-done.1, f32[512,512]{1,0:T(8,128)} %bitcast.31), custom_call_target="tpu_custom_call" | custom-call | flops 8589934592 | bytes 8388608 | tf_op jit(solution)/shard_map/assemble_strip/pallas_call | solution.py:461
  76.8 6.4 %all-to-all-done.1.got = bf16[128,80,128]{2,1,0:T(8,128)(2,1)S(1)} async-done(((bf16[128,80,128]{2,1,0:T(8,128)(2,1)}), bf16[128,80,128]{2,1,0:T(8,128)(2,1)S(1)}, u32[]{:S(2)}, u32[]{:S(2)}) %all-to-all-start.1) | async-done | bytes 2621472 | tf_op jit(solution)/shard_map/all_to_all | solution.py:22
  83.2 2.0 %upper_rows.1.upper.mine = bf16[512,512]{1,0:T(8,128)(2,1)S(1)} custom-call(bf16[128,80,128]{2,1,0:T(8,128)(2,1)S(1)} %all-to-all-done.1.got, bf16[80,1024,256]{2,1,0:T(8,128)(2,1)} %assemble_strip.1.blocks), custom_call_target="tpu_custom_call" | custom-call | flops 536870912 | bytes 2097152 | tf_op jit(solution)/shard_map/upper_rows/pallas_call | solution.py:477
  85.3 0.9 collective-permute-start.1
  86.2 2.2 %fetch_blocks.1.before = bf16[8,1024,256]{2,1,0:T(8,128)(2,1)S(1)} custom-call(bf16[80,1024,256]{2,1,0:T(8,128)(2,1)} %assemble_strip.1.blocks, bf16[512,512]{1,0:T(8,128)(2,1)S(1)} %upper_rows.1.upper.mine), custom_call_target="tpu_custom_call" | custom-call | bytes 8388608 | tf_op jit(solution)/shard_map/fetch_blocks/pallas_call | solution.py:494
  88.4 0.0 collective-permute-done.1.theirs
  88.4 2.9 %update_blocks.1 = (bf16[8,1024,256]{2,1,0:T(8,128)(2,1)S(1)}, bf16[64,512]{1,0:T(8,128)(2,1)}) custom-call(bf16[128,80,128]{2,1,0:T(8,128)(2,1)S(1)} %all-to-all-done.1.got, bf16[512,512]{1,0:T(8,128)(2,1)S(1)} %upper_rows.1.upper.mine, bf16[512,512]{1,0:T(8,128)(2,1)S(1)} %collective-permute-done.1.theirs, bf16[8,1024,256]{2,1,0:T(8,128)(2,1)S(1)} %fetch_blocks.1.before), custom_call_target="tpu_custom_call" | custom-call | flops 2147483648 | bytes 12582912 | tf_op jit(solution)/shard_map/update_blocks/pallas_call | solution.py:504
  91.4 56.2 %all_to_all.15.got = bf16[128,64,256]{2,1,0:T(8,128)(2,1)S(1)} all-to-all(bf16[128,64,256]{2,1,0:T(8,128)(2,1)S(1)} %bitcast.29), channel_id=1, replica_groups=mesh['row'=8,'col'=16] {'row','col'}, dimensions={0} | all-to-all | bytes 8388608 | tf_op jit(solution)/shard_map/all_to_all | solution.py:22
  147.5 3.4 %widen_blocks.1 = f32[64,32768]{1,0:T(8,128)} custom-call(bf16[128,64,256]{2,1,0:T(8,128)(2,1)S(1)} %all_to_all.15.got), custom_call_target="tpu_custom_call" | custom-call | flops 2097152 | bytes 12582912 | tf_op jit(solution)/shard_map/widen_blocks/pallas_call | solution.py:519
  (1 shorter events, 0.0 us)
Async XLA Ops:
  4.9 32.8 %all-to-all-start = ((bf16[128,40,128]{2,1,0:T(8,128)(2,1)}), bf16[128,40,128]{2,1,0:T(8,128)(2,1)S(1)}, u32[]{:S(2)}, u32[]{:S(2)}) async-start(bf16[128,40,128]{2,1,0:T(8,128)(2,1)} %pick_pivots.1), calls=%async_computation | async-start | bytes 2621440 | tf_op jit(solution)/shard_map/all_to_all | solution.py:22
  22.1 17.2 %copy-start.6 = (f32[64]{0:T(128)S(1)}, f32[64]{0:T(128)}, u32[]{:S(2)}) copy-start(f32[64]{0:T(128)} %param.15) | copy-start | bytes 772
  22.2 17.2 %copy-start.2 = (f32[16,512]{1,0:T(8,128)S(1)}, f32[16,512]{1,0:T(8,128)}, u32[]{:S(2)}) copy-start(f32[16,512]{1,0:T(8,128)} %kernels_at.1) | copy-start | bytes 98308
  37.8 5.9 %copy-start = (bf16[128,40,128]{2,1,0:T(8,128)(2,1)}, bf16[128,40,128]{2,1,0:T(8,128)(2,1)S(1)}, u32[]{:S(2)}) copy-start(bf16[128,40,128]{2,1,0:T(8,128)(2,1)S(1)} %all-to-all-done.got) | copy-start | bytes 3932164
  37.8 4.2 %collective-permute-start = (bf16[128,40,128]{2,1,0:T(8,128)(2,1)S(1)}, bf16[128,40,128]{2,1,0:T(8,128)(2,1)S(1)}, u32[]{:S(2)}, u32[]{:S(2)}) collective-permute-start(bf16[128,40,128]{2,1,0:T(8,128)(2,1)S(1)} %all-to-all-done.got), channel_id=1, source_target_pairs={{0,16},{16,0},{32,48},{48,32},{64,80},{80,64},{96,112},{112,96},{1... | collective-permute-start | bytes 3932168 | tf_op jit(solution)/shard_map/ppermute | solution.py:419
  42.0 1.7 %copy-start.1 = (bf16[128,40,128]{2,1,0:T(8,128)(2,1)}, bf16[128,40,128]{2,1,0:T(8,128)(2,1)S(1)}, u32[]{:S(2)}) copy-start(bf16[128,40,128]{2,1,0:T(8,128)(2,1)S(1)} %collective-permute-done.other) | copy-start | bytes 3932164
  43.7 4.0 %copy-start.3 = (s32[32,16,8]{0,2,1:T(8,128)S(1)}, s32[32,16,8]{0,2,1:T(8,128)}, u32[]{:S(2)}) copy-start(s32[32,16,8]{0,2,1:T(8,128)} %param.13) | copy-start | bytes 49156
  43.7 5.7 %copy-start.4 = (s32[32,16,8]{0,2,1:T(8,128)S(1)}, s32[32,16,8]{0,2,1:T(8,128)}, u32[]{:S(2)}) copy-start(s32[32,16,8]{0,2,1:T(8,128)} %param.12) | copy-start | bytes 49156
  43.7 5.7 %copy-start.5 = (s32[32,16]{0,1:T(8,128)S(1)}, s32[32,16]{0,1:T(8,128)}, u32[]{:S(2)}) copy-start(s32[32,16]{0,1:T(8,128)} %param.14) | copy-start | bytes 6148
  43.7 39.5 %all-to-all-start.1 = ((bf16[128,80,128]{2,1,0:T(8,128)(2,1)}), bf16[128,80,128]{2,1,0:T(8,128)(2,1)S(1)}, u32[]{:S(2)}, u32[]{:S(2)}) async-start(bf16[128,80,128]{2,1,0:T(8,128)(2,1)} %chosen_rows.1), calls=%async_computation.1 | async-start | bytes 5242880 | tf_op jit(solution)/shard_map/all_to_all | solution.py:22
  85.3 3.2 %collective-permute-start.1 = (bf16[512,512]{1,0:T(8,128)(2,1)S(1)}, bf16[512,512]{1,0:T(8,128)(2,1)S(1)}, u32[]{:S(2)}, u32[]{:S(2)}) collective-permute-start(bf16[512,512]{1,0:T(8,128)(2,1)S(1)} %upper_rows.1.upper.mine), channel_id=1, source_target_pairs={{0,16},{16,0},{32,48},{48,32},{64,80},{80,64},{96,112},{112,96},{1... | collective-permute-start | bytes 1572872 | tf_op jit(solution)/shard_map/ppermute | solution.py:493

commit v7 on v5

--- a/solution.py
+++ b/solution.py
@@ -323,8 +323,11 @@
             got[p * ncol : (p + 1) * ncol, b * deep : (b + 1) * deep, :].reshape(npiv, LANES)
             for b in range(wide // LANES)
         ]
-        change = jnp.dot(upper_all[...], jnp.concatenate(pieces, axis=1), preferred_element_type=F32)
-        out[p] = (before[p].astype(F32) - change).astype(BF16)
+        columns = jnp.concatenate(pieces, axis=1)
+        for upper, side in ((mine, core), (theirs, 1 - core)):
+            span = pl.ds(pl.multiple_of(side * half, half), half)
+            change = jnp.dot(upper[...], columns, preferred_element_type=F32)
+            out[p, span, :] = (before[p, span, :].astype(F32) - change).astype(BF16)
 
 
 def widen_kernel(got, out, broad, sent):

time: 152 us -> 152 us (level)
  no operation moved by 1% of the time
where the time goes in v7:
time: 152 us; the launch traced here: 151 us
  blocking collectives  56.2 us (37%)
  Pallas kernels  33.2 us (22%)
  waiting for transfers between devices  21.9 us (14%)
  starting transfers between devices  17.9 us (12%)
  local copies, waits for them, and re-layouts  17.6 us (12%)
  matrix products  1.96 us (1%)
    all_to_all x1, blocking collectives, exchange(): return lax.all_to_all(chunks, ALL, split_axis=0, concat_axis=0, tiled=True)  56.2 us
    all_to_all x2, waiting for transfers between devices, exchange(): return lax.all_to_all(chunks, ALL, split_axis=0, concat_axis=0, tiled=True)  20.3 us
    pallas_call x1, Pallas kernels, shards(): pl.pallas_call(assemble_kernel, out_shape=jax.ShapeDtypeStruct((slots, sc...  15.5 us
    all_to_all x2, starting transfers between devices, exchange(): return lax.all_to_all(chunks, ALL, split_axis=0, concat_axis=0, tiled=True)  15.5 us
    reshape x2, local copies, waits for them, and re-layouts, shards(): panel.reshape(deep, ndev, wide // LANES, LANES).transpose(1, 2, 0, 3)  5.68 us
    unnamed x17, local copies, waits for them, and re-layouts  5.04 us
    pallas_call x1, Pallas kernels, shards(): pl.pallas_call(functools.partial(pick_kernel, own), out_shape=jax.ShapeDt...  4.35 us
    pallas_call x1, Pallas kernels, shards(): pl.pallas_call(widen_kernel, out_shape=jax.ShapeDtypeStruct((width, ndev...  3.45 us
  transfers between devices with their start and end apart: 4, of which 3 were waited for; matrix products, arithmetic and copies ran while one was open for 14% of the time, Pallas kernels for 12%

profile of v7, /device:TPU:1, one launch (start us, length us, event | category | flops | bytes accessed | tf_op | source)
XLA Modules:
  0.0 151.3 jit_solution(6069666295151747919)
XLA Ops:
  0.6 4.4 %pick_pivots.1 = bf16[128,40,128]{2,1,0:T(8,128)(2,1)} custom-call(s32[1,512]{1,0:T(1,128)} %bitcast.41, s32[128,32]{1,0:T(8,128)} %bitcast.38, s32[128,32]{1,0:T(8,128)} %bitcast.37, s32[16,32]{1,0:T(8,128)} %bitcast.39, bf16[2048,512]{1,0:T(8,128)(2,1)} %bitcast.34, bf16[1,64,512]{2,1,0:T(8,128)(2,1)} %form_strip_at.1), custom_call_target="tpu_custom_call" | custom-call | flops 1073741824 | bytes 4194304 | tf_op jit(solution)/shard_map/pick_pivots/pallas_call | solution.py:381
  5.0 11.5 %all-to-all-start = ((bf16[128,40,128]{2,1,0:T(8,128)(2,1)}), bf16[128,40,128]{2,1,0:T(8,128)(2,1)S(1)}, u32[]{:S(2)}, u32[]{:S(2)}) async-start(bf16[128,40,128]{2,1,0:T(8,128)(2,1)} %pick_pivots.1), calls=%async_computation | async-start | bytes 2621440 | tf_op jit(solution)/shard_map/all_to_all | solution.py:22
  16.5 3.2 %reshape.42 = bf16[32,128,2,128]{3,2,1,0:T(2,128)(2,1)S(1)} reshape(bf16[32,32768]{1,0:T(8,128)(2,1)} %param.19) | data formatting | bytes 4194304 | tf_op jit(solution)/shard_map/reshape | solution.py:412
  19.8 2.4 %copy.31 = bf16[32,128,2,128]{3,0,2,1:T(8,128)(2,1)S(1)} copy(bf16[32,128,2,128]{3,2,1,0:T(2,128)(2,1)S(1)} %reshape.42) | data formatting | bytes 4194304 | tf_op jit(solution)/shard_map/reshape | solution.py:412
  22.2 0.0 copy-start.6
  22.2 0.0 copy-start.2
  22.2 1.7 %pad.4.kept = bf16[128,80,128]{2,1,0:T(8,128)(2,1)} pad(bf16[128,64,128]{2,1,0:T(8,128)(2,1)S(1)} %bitcast.30, bf16[]{:T(256)} %constant.6.clone.1), padding=0_0x0_16x0_0 | pad | bytes 4718594 | tf_op jit(solution)/shard_map/jit(_pad)/pad | solution.py:415
  23.9 13.9 %all-to-all-done.got = bf16[128,40,128]{2,1,0:T(8,128)(2,1)S(1)} async-done(((bf16[128,40,128]{2,1,0:T(8,128)(2,1)}), bf16[128,40,128]{2,1,0:T(8,128)(2,1)S(1)}, u32[]{:S(2)}, u32[]{:S(2)}) %all-to-all-start) | async-done | bytes 1310752 | tf_op jit(solution)/shard_map/all_to_all | solution.py:22
  37.8 0.0 copy-start
  37.8 1.5 collective-permute-start
  39.3 0.0 copy-done.6
  39.3 0.1 copy.32.angular_at
  39.4 0.0 copy-done.2
  39.4 1.0 scale_pivots.1.scaled
  40.4 1.6 %collective-permute-done.other = bf16[128,40,128]{2,1,0:T(8,128)(2,1)S(1)} collective-permute-done((bf16[128,40,128]{2,1,0:T(8,128)(2,1)S(1)}, bf16[128,40,128]{2,1,0:T(8,128)(2,1)S(1)}, u32[]{:S(2)}, u32[]{:S(2)}) %collective-permute-start) | collective-permute-done | bytes 1310752 | tf_op jit(solution)/shard_map/ppermute | solution.py:418
  42.0 0.0 copy-start.1
  42.0 1.7 %chosen_rows.1 = bf16[128,80,128]{2,1,0:T(8,128)(2,1)} custom-call(bf16[128,40,128]{2,1,0:T(8,128)(2,1)S(1)} %all-to-all-done.got, bf16[128,40,128]{2,1,0:T(8,128)(2,1)S(1)} %collective-permute-done.other, bf16[64,512]{1,0:T(8,128)(2,1)S(1)} %scale_pivots.1.scaled, bf16[128,80,128]{2,1,0:T(8,128)(2,1)} %pad.4.kept), custom_call_target="tpu_custom_call", output_to_operand_aliasing={{}: (3, {})} | custom-call | flops 67108864 | bytes 4194304 | tf_op jit(solution)/shard_map/chosen_rows/pallas_call | solution.py:436
  43.7 0.0 copy-done
  43.7 0.0 copy-done.1
  43.7 0.0 copy-start.3
  43.7 0.0 copy-start.4
  43.7 0.0 copy-start.5
  43.8 4.0 %all-to-all-start.1 = ((bf16[128,80,128]{2,1,0:T(8,128)(2,1)}), bf16[128,80,128]{2,1,0:T(8,128)(2,1)S(1)}, u32[]{:S(2)}, u32[]{:S(2)}) async-start(bf16[128,80,128]{2,1,0:T(8,128)(2,1)} %chosen_rows.1), calls=%async_computation.1 | async-start | bytes 5242880 | tf_op jit(solution)/shard_map/all_to_all | solution.py:22
  47.8 0.0 copy-done.3
  47.8 0.2 copy.33
  47.9 1.3 select_reduce_fusion
  49.3 0.2 copy.34
  49.4 0.0 copy-done.4
  49.4 0.0 copy-done.5
  49.5 0.1 select_reduce_fusion.1
  49.6 0.2 copy.35
  49.8 2.6 %copy.36 = f32[512,512]{0,1:T(8,128)} copy(f32[512,512]{1,0:T(8,128)} %param.18) | data formatting | bytes 2097152 | tf_op args[8]
  52.4 2.5 %reshape.45 = f32[512,128,4]{0,2,1:T(4,128)} reshape(f32[512,512]{0,1:T(8,128)} %copy.36) | data formatting | bytes 2097152 | tf_op jit(solution)/shard_map/reshape | solution.py:458
  54.9 2.3 %copy.37 = f32[512,4,128]{2,1,0:T(4,128)} copy(f32[512,4,128]{0,1,2:T(4,128)} %bitcast.32) | data formatting | bytes 2097152 | tf_op jit(solution)/shard_map/transpose | solution.py:458
  57.1 2.2 %copy.41 = f32[64,8,4,128]{3,1,2,0:T(8,128)} copy(f32[64,8,4,128]{3,2,1,0:T(4,128)} %bitcast.33) | data formatting | bytes 2097152
  59.4 2.0 %fusion.1.radial = f32[4,8,16,512]{3,2,1,0:T(8,128)} fusion(f32[4,8,16,16]{3,2,1,0:T(8,128)S(1)} %bitcast.36, f32[16,512]{1,0:T(8,128)S(1)} %copy-done.2), kind=kOutput, calls=%fused_computation.7 | convolution fusion | flops 50331648 | bytes 1114112 | tf_op jit(solution)/shard_map/dot_general | solution.py:38
  61.3 15.5 %assemble_strip.1.blocks = bf16[80,1024,256]{2,1,0:T(8,128)(2,1)} custom-call(bf16[4,8,64,512]{3,2,1,0:T(8,128)(2,1)} %bitcast.35, f32[4,8,16,512]{3,2,1,0:T(8,128)} %fusion.1.radial, bf16[128,40,128]{2,1,0:T(8,128)(2,1)} %copy-done, bf16[128,40,128]{2,1,0:T(8,128)(2,1)} %copy-done.1, f32[512,512]{1,0:T(8,128)} %bitcast.31), custom_call_target="tpu_custom_call" | custom-call | flops 8589934592 | bytes 8388608 | tf_op jit(solution)/shard_map/assemble_strip/pallas_call | solution.py:460
  76.8 6.4 %all-to-all-done.1.got = bf16[128,80,128]{2,1,0:T(8,128)(2,1)S(1)} async-done(((bf16[128,80,128]{2,1,0:T(8,128)(2,1)}), bf16[128,80,128]{2,1,0:T(8,128)(2,1)S(1)}, u32[]{:S(2)}, u32[]{:S(2)}) %all-to-all-start.1) | async-done | bytes 2621472 | tf_op jit(solution)/shard_map/all_to_all | solution.py:22
  83.3 2.0 %upper_rows.1.upper.mine = bf16[512,512]{1,0:T(8,128)(2,1)S(1)} custom-call(bf16[128,80,128]{2,1,0:T(8,128)(2,1)S(1)} %all-to-all-done.1.got, bf16[80,1024,256]{2,1,0:T(8,128)(2,1)} %assemble_strip.1.blocks), custom_call_target="tpu_custom_call" | custom-call | flops 536870912 | bytes 2097152 | tf_op jit(solution)/shard_map/upper_rows/pallas_call | solution.py:476
  85.3 0.9 collective-permute-start.1
  86.3 2.2 %fetch_blocks.1.before = bf16[8,1024,256]{2,1,0:T(8,128)(2,1)S(1)} custom-call(bf16[80,1024,256]{2,1,0:T(8,128)(2,1)} %assemble_strip.1.blocks, bf16[512,512]{1,0:T(8,128)(2,1)S(1)} %upper_rows.1.upper.mine), custom_call_target="tpu_custom_call" | custom-call | bytes 8388608 | tf_op jit(solution)/shard_map/fetch_blocks/pallas_call | solution.py:493
  88.5 0.0 collective-permute-done.1.theirs
  88.5 3.0 %update_blocks.1 = (bf16[8,1024,256]{2,1,0:T(8,128)(2,1)S(1)}, bf16[64,512]{1,0:T(8,128)(2,1)}) custom-call(bf16[128,80,128]{2,1,0:T(8,128)(2,1)S(1)} %all-to-all-done.1.got, bf16[512,512]{1,0:T(8,128)(2,1)S(1)} %upper_rows.1.upper.mine, bf16[512,512]{1,0:T(8,128)(2,1)S(1)} %collective-permute-done.1.theirs, bf16[8,1024,256]{2,1,0:T(8,128)(2,1)S(1)} %fetch_blocks.1.before), custom_call_target="tpu_custom_call" | custom-call | flops 2147483648 | bytes 12582912 | tf_op jit(solution)/shard_map/update_blocks/pallas_call | solution.py:503
  91.5 56.2 %all_to_all.15.got = bf16[128,64,256]{2,1,0:T(8,128)(2,1)S(1)} all-to-all(bf16[128,64,256]{2,1,0:T(8,128)(2,1)S(1)} %bitcast.29), channel_id=1, replica_groups=mesh['row'=8,'col'=16] {'row','col'}, dimensions={0} | all-to-all | bytes 8388608 | tf_op jit(solution)/shard_map/all_to_all | solution.py:22
  147.7 3.4 %widen_blocks.1 = f32[64,32768]{1,0:T(8,128)} custom-call(bf16[128,64,256]{2,1,0:T(8,128)(2,1)S(1)} %all_to_all.15.got), custom_call_target="tpu_custom_call" | custom-call | flops 2097152 | bytes 12582912 | tf_op jit(solution)/shard_map/widen_blocks/pallas_call | solution.py:518
  (1 shorter events, 0.0 us)
Async XLA Ops:
  5.0 32.8 %all-to-all-start = ((bf16[128,40,128]{2,1,0:T(8,128)(2,1)}), bf16[128,40,128]{2,1,0:T(8,128)(2,1)S(1)}, u32[]{:S(2)}, u32[]{:S(2)}) async-start(bf16[128,40,128]{2,1,0:T(8,128)(2,1)} %pick_pivots.1), calls=%async_computation | async-start | bytes 2621440 | tf_op jit(solution)/shard_map/all_to_all | solution.py:22
  22.2 17.2 %copy-start.6 = (f32[64]{0:T(128)S(1)}, f32[64]{0:T(128)}, u32[]{:S(2)}) copy-start(f32[64]{0:T(128)} %param.15) | copy-start | bytes 772
  22.2 17.2 %copy-start.2 = (f32[16,512]{1,0:T(8,128)S(1)}, f32[16,512]{1,0:T(8,128)}, u32[]{:S(2)}) copy-start(f32[16,512]{1,0:T(8,128)} %kernels_at.1) | copy-start | bytes 98308
  37.8 5.9 %copy-start = (bf16[128,40,128]{2,1,0:T(8,128)(2,1)}, bf16[128,40,128]{2,1,0:T(8,128)(2,1)S(1)}, u32[]{:S(2)}) copy-start(bf16[128,40,128]{2,1,0:T(8,128)(2,1)S(1)} %all-to-all-done.got) | copy-start | bytes 3932164
  37.8 4.2 %collective-permute-start = (bf16[128,40,128]{2,1,0:T(8,128)(2,1)S(1)}, bf16[128,40,128]{2,1,0:T(8,128)(2,1)S(1)}, u32[]{:S(2)}, u32[]{:S(2)}) collective-permute-start(bf16[128,40,128]{2,1,0:T(8,128)(2,1)S(1)} %all-to-all-done.got), channel_id=1, source_target_pairs={{0,16},{16,0},{32,48},{48,32},{64,80},{80,64},{96,112},{112,96},{1... | collective-permute-start | bytes 3932168 | tf_op jit(solution)/shard_map/ppermute | solution.py:418
  42.0 1.7 %copy-start.1 = (bf16[128,40,128]{2,1,0:T(8,128)(2,1)}, bf16[128,40,128]{2,1,0:T(8,128)(2,1)S(1)}, u32[]{:S(2)}) copy-start(bf16[128,40,128]{2,1,0:T(8,128)(2,1)S(1)} %collective-permute-done.other) | copy-start | bytes 3932164
  43.7 4.0 %copy-start.3 = (s32[32,16,8]{0,2,1:T(8,128)S(1)}, s32[32,16,8]{0,2,1:T(8,128)}, u32[]{:S(2)}) copy-start(s32[32,16,8]{0,2,1:T(8,128)} %param.13) | copy-start | bytes 49156
  43.7 5.7 %copy-start.4 = (s32[32,16,8]{0,2,1:T(8,128)S(1)}, s32[32,16,8]{0,2,1:T(8,128)}, u32[]{:S(2)}) copy-start(s32[32,16,8]{0,2,1:T(8,128)} %param.12) | copy-start | bytes 49156
  43.7 5.7 %copy-start.5 = (s32[32,16]{0,1:T(8,128)S(1)}, s32[32,16]{0,1:T(8,128)}, u32[]{:S(2)}) copy-start(s32[32,16]{0,1:T(8,128)} %param.14) | copy-start | bytes 6148
  43.8 39.5 %all-to-all-start.1 = ((bf16[128,80,128]{2,1,0:T(8,128)(2,1)}), bf16[128,80,128]{2,1,0:T(8,128)(2,1)S(1)}, u32[]{:S(2)}, u32[]{:S(2)}) async-start(bf16[128,80,128]{2,1,0:T(8,128)(2,1)} %chosen_rows.1), calls=%async_computation.1 | async-start | bytes 5242880 | tf_op jit(solution)/shard_map/all_to_all | solution.py:22
  85.3 3.2 %collective-permute-start.1 = (bf16[512,512]{1,0:T(8,128)(2,1)S(1)}, bf16[512,512]{1,0:T(8,128)(2,1)S(1)}, u32[]{:S(2)}, u32[]{:S(2)}) collective-permute-start(bf16[512,512]{1,0:T(8,128)(2,1)S(1)} %upper_rows.1.upper.mine), channel_id=1, source_target_pairs={{0,16},{16,0},{32,48},{48,32},{64,80},{80,64},{96,112},{112,96},{1... | collective-permute-start | bytes 1572872 | tf_op jit(solution)/shard_map/ppermute | solution.py:492
